TPU v7x, 512 devices: a whole 4x4x16 slice. The times are simulated.
512 devices in a mesh: gx: 8 (over x, core), gy: 4 (over y), gz: 16 (over z).
Axes of the slice: x: 4, y: 4, z: 16, core: 2. Of those that a mesh axis runs over, the one named last changes fastest.
Arguments:
- positions: float32 [16, 4, 16, 3, 128], P('gx', 'gy', 'gz'), may hold values from 0 to 11, as said below
- polarity: float32 [16, 4, 16, 128], P('gx', 'gy', 'gz'), may hold values from 0.3 to 2.5
- perm_field: float32 [16, 4, 16, 3, 128], P('gx', 'gy', 'gz'), may hold values from -6 to 6
- groups: int32 [16, 4, 16, 128], P('gx', 'gy', 'gz'), may hold values from 0 to 7
- occupancy: int32 [16, 4, 16], P('gx', 'gy', 'gz'), may hold values from 64 to 128, as said below
Outputs:
- dipoles: float32 [16, 4, 16, 3, 128], P('gx', 'gy', 'gz')
- residual: float32 [16, 4, 16, 3, 128], P('gx', 'gy', 'gz')
Inputs may be any that keep to these rules, and one draw needn't show every extreme that they name: `positions`: coordinates lie inside the atom's cell of edge 11; any two atoms of the box are at least 0.6 apart, across cell faces too. `occupancy`: some cells in every draw hold all 128 slots live; dead slots come last in a cell.
All inputs are finite; a program needn't handle non-finite values.
Results may differ from a plain program's by a relative error of at most 0.00035.
Values sent between devices are 32-bit elements; how exact they have to be, the bound alone decides.
A program may use at most 64 MiB of HBM per device.

v0:
```python
import jax
import jax.numpy as jnp
import numpy as np
from jax import lax
from jax.sharding import PartitionSpec as P

ITERS = 3


CELL_EDGE = 11.0
CUTOFF = 9.0
THOLE_A = 0.39
EDGE_PICKS = ((-1, 1, 0), (0, -1, 1), (1, 0, -1))


def shifted(value, axis, steps):
    count = lax.axis_size(axis)
    pairs = [(source, (source + steps) % count) for source in range(count)]
    return lax.ppermute(value, axis, pairs)


def extended(cells, sides, width):
    for axis, dim in sides:
        count = lax.axis_size(axis)
        head = lax.slice_in_dim(cells, 0, width, axis=dim)
        tail = lax.slice_in_dim(cells, cells.shape[dim] - width, cells.shape[dim], axis=dim)
        cells = jnp.concatenate(
            [
                lax.ppermute(tail, axis, [(i, (i + 1) % count) for i in range(count)]),
                cells,
                lax.ppermute(head, axis, [((i + 1) % count, i) for i in range(count)]),
            ],
            axis=dim,
        )
    return cells


def offset_table():
    offsets_list = []
    for offset_x in (-1, 0, 1):
        for offset_y in (-1, 0, 1):
            for offset_z in (-1, 0, 1):
                triple = (offset_x, offset_y, offset_z)
                if triple == (0, 0, 0):
                    continue
                total = offset_x + offset_y + offset_z
                if not (total > 0 or (total == 0 and triple in EDGE_PICKS)):
                    continue
                offsets_list.append(triple)
    return np.array(offsets_list, dtype=np.int32)


def coupling(separation, polar_home, polar_other, weight, on_diagonal):
    squared = jnp.sum(separation * separation, axis=-3)
    if on_diagonal:
        squared = squared + jnp.eye(squared.shape[-1], dtype=jnp.float32)
    distance = jnp.sqrt(squared)
    inverse = 1.0 / distance
    inverse_cube = inverse * inverse * inverse
    damping = (
        THOLE_A
        * squared
        * distance
        / jnp.sqrt(polar_home[..., :, None] * polar_other[..., None, :])
    )
    falloff = jnp.exp(-damping)
    screen_three = 1.0 - falloff
    screen_five = 1.0 - (1.0 + damping) * falloff
    tapering = jnp.square(jnp.maximum(1.0 - squared / (CUTOFF * CUTOFF), 0.0))
    factor = tapering * weight
    return (
        factor * screen_three * inverse_cube,
        3.0 * factor * screen_five * inverse_cube * inverse * inverse,
    )


def field_home(separation, coupling_three, coupling_five, source_other):
    project = jnp.sum(separation * source_other[..., :, None, :], axis=-3)
    radial = jnp.sum(
        coupling_five[..., None, :, :] * project[..., None, :, :] * separation, axis=-1
    )
    return radial - jnp.sum(
        coupling_three[..., None, :, :] * source_other[..., :, None, :], axis=-1
    )


def field_other(separation, coupling_three, coupling_five, source_home):
    project = jnp.sum(separation * source_home[..., :, :, None], axis=-3)
    radial = jnp.sum(
        coupling_five[..., None, :, :] * project[..., None, :, :] * separation, axis=-2
    )
    return radial - jnp.sum(coupling_three[..., None, :, :] * source_home[..., :, :, None], axis=-2)


def fold_back(spill):
    lower_rim = spill[:, :, 0]
    upper_rim = spill[:, :, -1]
    from_below = shifted(upper_rim, "gz", 1)
    from_above = shifted(lower_rim, "gz", -1)
    spill = spill[:, :, 1:-1]
    spill = spill.at[:, :, 0].add(from_below)
    spill = spill.at[:, :, -1].add(from_above)
    lower_rim = spill[:, 0]
    upper_rim = spill[:, -1]
    from_below = shifted(upper_rim, "gy", 1)
    from_above = shifted(lower_rim, "gy", -1)
    spill = spill[:, 1:-1]
    spill = spill.at[:, 0].add(from_below)
    spill = spill.at[:, -1].add(from_above)
    lower_rim = spill[0]
    upper_rim = spill[-1]
    from_below = shifted(upper_rim, "gx", 1)
    from_above = shifted(lower_rim, "gx", -1)
    spill = spill[1:-1]
    spill = spill.at[0].add(from_below)
    spill = spill.at[-1].add(from_above)
    return spill


def squares(vector):
    return lax.psum(jnp.sum(vector * vector), ("gx", "gy", "gz"))


def shards(positions, polarity, perm_field, groups, occupancy):
    live = (lax.broadcasted_iota(jnp.int32, groups.shape, 3) < occupancy[..., None]).astype(
        jnp.float32
    )
    zero_index = jnp.zeros((), jnp.int32)
    padded_where, padded_polar = (
        extended(positions, (("gx", 0), ("gy", 1), ("gz", 2)), 1),
        extended(polarity, (("gx", 0), ("gy", 1), ("gz", 2)), 1),
    )
    self_sep = positions[..., None, :] - positions[..., :, None]
    self_weight = (groups[..., :, None] != groups[..., None, :]).astype(jnp.float32)
    self_three, self_five = coupling(self_sep, polarity, polarity, self_weight, True)
    residual = live[..., None, :] * perm_field
    dipoles = jnp.zeros_like(residual)
    direction = residual
    norm_now = squares(residual)
    for iteration in range(ITERS):
        vector = direction
        padded_dip = extended(vector, (("gx", 0), ("gy", 1), ("gz", 2)), 1)
        own_field = field_home(self_sep, self_three, self_five, vector)

        def partner(offset):
            corner = offset + 1
            start_five = (corner[0], corner[1], corner[2], zero_index, zero_index)
            start_four = (corner[0], corner[1], corner[2], zero_index)
            where_other = lax.dynamic_slice(padded_where, start_five, positions.shape)
            where_other = where_other + offset.astype(jnp.float32)[:, None] * CELL_EDGE
            polar_other = lax.dynamic_slice(padded_polar, start_four, polarity.shape)
            source_other = lax.dynamic_slice(padded_dip, start_five, vector.shape)
            separation = where_other[..., None, :] - positions[..., :, None]
            coupling_three, coupling_five = coupling(separation, polarity, polar_other, 1.0, False)
            return (separation, coupling_three, coupling_five, source_other, start_five)

        offsets = jnp.asarray(offset_table())

        def visit_half(carried, offset):
            field_sum, spill = carried
            separation, coupling_three, coupling_five, source_other, start_five = partner(offset)
            field_sum = field_sum + field_home(
                separation, coupling_three, coupling_five, source_other
            )
            returned = field_other(separation, coupling_three, coupling_five, vector)
            current = lax.dynamic_slice(spill, start_five, vector.shape)
            spill = lax.dynamic_update_slice(spill, current + returned, start_five)
            return ((field_sum, spill), None)

        (field_sum, spill), unused = lax.scan(
            visit_half, (own_field, jnp.zeros_like(padded_dip)), offsets
        )
        field_sum = field_sum + fold_back(spill)
        applied = live[..., None, :] * (vector / polarity[..., None, :] - field_sum)
        curve = lax.psum(jnp.sum(direction * applied), ("gx", "gy", "gz"))
        step_size = norm_now / curve
        dipoles = dipoles + step_size * direction
        residual = residual - step_size * applied
        if iteration + 1 < ITERS:
            norm_next = squares(residual)
            direction = residual + norm_next / norm_now * direction
            norm_now = norm_next
    return (dipoles, residual)


def solution(mesh):
    return jax.shard_map(
        shards,
        mesh=mesh,
        in_specs=(
            P("gx", "gy", "gz", None, None),
            P("gx", "gy", "gz", None),
            P("gx", "gy", "gz", None, None),
            P("gx", "gy", "gz", None),
            P("gx", "gy", "gz"),
        ),
        out_specs=(P("gx", "gy", "gz", None, None), P("gx", "gy", "gz", None, None)),
        check_vma=False,
    )
```

profile of v0, /device:TPU:1, one launch (start us, length us, event | category | flops | bytes accessed | tf_op | source)
XLA Modules:
  0.0 1053.8 jit_solution(16802423810953654048)
XLA Ops:
  4.0 4.3 collective-permute-start.13
  8.3 2.9 collective-permute-start.7
  13.1 3.0 collective-permute-start.1
  18.1 4.6 collective-permute-start.9
  24.6 4.6 collective-permute-start.15
  31.2 4.6 collective-permute-start.3
  37.7 5.8 collective-permute-start.11
  45.5 4.6 collective-permute-start.17
  52.1 4.6 collective-permute-start.5
  57.6 118.6 %while.57 = (s32[]{:T(128)}, f32[2,1,1,3,128]{4,3,0,2,1:T(4,128)S(1)}, f32[4,3,3,3,128]{4,3,0,2,1:T(4,128)S(1)}, f32[4,3,3,3,128]{4,3,0,2,1:T(4,128)S(1)}, f32[2...) while((s32[]{:T(128)}, ...), condition=%wide.region_14.15_spmd.clone, body=%wide.region_6.14_spmd.sunk.clone.sunk | while | flops 2786068 | bytes 1804663 | solution.py:170
  178.2 4.8 collective-permute-start.19
  185.9 4.6 collective-permute-start.21
  191.2 6.3 collective-permute-start.22
  201.5 109.2 %all-reduce = (f32[]{:T(128)}, f32[]{:T(128)}) all-reduce(f32[]{:T(128)} %get-tuple-element.585, f32[]{:T(128)} %get-tuple-element.584), channel_id=1, replica_groups=mesh['gx'=8,'gy'=4,'gz'=16] {'gx','gy','gz'}, use_global_device_ids=true, to_apply=%region_1.0 | all-reduce | flops 2 | bytes 16 | tf_op jit(solution)/shard_map/psum | solution.py:121
  312.7 98.7 %psum.44 = f32[]{:T(128)} all-reduce(f32[]{:T(128)} %multiply_reduce_fusion.12), channel_id=1, replica_groups=mesh['gx'=8,'gy'=4,'gz'=16] {'gx','gy','gz'}, use_global_device_ids=true, to_apply=%region_18.19 | all-reduce | flops 1 | bytes 8 | tf_op jit(solution)/shard_map/psum | solution.py:121
  418.3 4.6 collective-permute-start.27
  423.6 3.7 collective-permute-start.28
  427.3 2.8 collective-permute-start.29
  432.2 118.6 %while.58 = (s32[]{:T(128)}, f32[2,1,1,3,128]{4,3,0,2,1:T(4,128)S(1)}, f32[4,3,3,3,128]{4,3,0,2,1:T(4,128)S(1)}, f32[4,3,3,3,128]{4,3,0,2,1:T(4,128)S(1)}, f32[2...) while((s32[]{:T(128)}, ...), condition=%wide.region_30.0_spmd.clone, body=%wide.region_22.30_spmd.sunk.clone.sunk | while | flops 2786068 | bytes 1804663 | solution.py:170
  552.8 4.6 collective-permute-start.31
  560.7 4.1 collective-permute-start.33
  565.6 4.9 collective-permute-start.34
  574.1 107.2 %psum.45 = f32[]{:T(128)} all-reduce(f32[]{:T(128)} %get-tuple-element.646), channel_id=1, replica_groups=mesh['gx'=8,'gy'=4,'gz'=16] {'gx','gy','gz'}, use_global_device_ids=true, to_apply=%region_32.0 | all-reduce | flops 1 | bytes 8 | tf_op jit(solution)/shard_map/psum | solution.py:175
  683.3 98.6 %psum.46 = f32[]{:T(128)} all-reduce(f32[]{:T(128)} %get-tuple-element.644), channel_id=1, replica_groups=mesh['gx'=8,'gy'=4,'gz'=16] {'gx','gy','gz'}, use_global_device_ids=true, to_apply=%region_34.0 | all-reduce | flops 1 | bytes 8 | tf_op jit(solution)/shard_map/psum | solution.py:121
  789.2 4.6 collective-permute-start.39
  794.5 3.7 collective-permute-start.40
  798.2 2.8 collective-permute-start.41
  803.1 118.6 %while.59 = (s32[]{:T(128)}, f32[2,1,1,3,128]{4,3,0,2,1:T(4,128)S(1)}, f32[4,3,3,3,128]{4,3,0,2,1:T(4,128)S(1)}, f32[4,3,3,3,128]{4,3,0,2,1:T(4,128)S(1)}, f32[2...) while((s32[]{:T(128)}, ...), condition=%wide.region_46.47_spmd.clone, body=%wide.region_38.46_spmd.sunk.clone.sunk | while | flops 2786068 | bytes 1804663 | solution.py:170
  923.7 4.6 collective-permute-start.43
  931.2 4.7 collective-permute-start.45
  936.7 4.3 collective-permute-start.46
  944.6 107.2 %psum.47 = f32[]{:T(128)} all-reduce(f32[]{:T(128)} %get-tuple-element.642), channel_id=1, replica_groups=mesh['gx'=8,'gy'=4,'gz'=16] {'gx','gy','gz'}, use_global_device_ids=true, to_apply=%region_48.49 | all-reduce | flops 1 | bytes 8 | tf_op jit(solution)/shard_map/psum | solution.py:175
  (727 shorter events, 196.2 us)
Async XLA Ops:
  1.4 16.7 %collective-permute-start.12 = (f32[1,1,1,3,128]{4,2,3,1,0:T(1,128)S(1)}, f32[1,1,1,3,128]{4,2,3,1,0:T(1,128)S(1)}, u32[]{:S(2)}, u32[]{:S(2)}) collective-permute-start(f32[1,1,1,3,128]{4,2,3,1,0:T(1,128)S(1)} %get-tuple-element.694), channel_id=1, source_target_pairs={{0,64},{64,128},{128,192},{192,256},{256,320},{320,384},{384,448},... | collective-permute-start | bytes 4616 | tf_op jit(solution)/shard_map/ppermute | solution.py:29
  4.0 18.6 %collective-permute-start.13 = (f32[1,1,1,3,128]{4,2,3,1,0:T(1,128)S(1)}, f32[1,1,1,3,128]{4,2,3,1,0:T(1,128)S(1)}, u32[]{:S(2)}, u32[]{:S(2)}) collective-permute-start(f32[1,1,1,3,128]{4,2,3,1,0:T(1,128)S(1)} %get-tuple-element.695), channel_id=1, source_target_pairs={{64,0},{128,64},{192,128},{256,192},{320,256},{384,320},{448,384},... | collective-permute-start | bytes 4616 | tf_op jit(solution)/shard_map/ppermute | solution.py:31
  8.3 7.8 collective-permute-start.7
  11.3 13.3 %collective-permute-start = (f32[1,1,1,3,128]{4,3,0,2,1:T(4,128)S(1)}, f32[1,1,1,3,128]{4,3,0,2,1:T(4,128)S(1)}, u32[]{:S(2)}, u32[]{:S(2)}) collective-permute-start(f32[1,1,1,3,128]{4,3,0,2,1:T(4,128)S(1)} %copy.153), channel_id=1, source_target_pairs={{0,64},{64,128},{128,192},{192,256},{256,320},{320,384},{384,448},... | collective-permute-start | bytes 4616 | tf_op jit(solution)/shard_map/ppermute | solution.py:29
  13.1 16.1 %collective-permute-start.1 = (f32[1,1,1,3,128]{4,3,0,2,1:T(4,128)S(1)}, f32[1,1,1,3,128]{4,3,0,2,1:T(4,128)S(1)}, u32[]{:S(2)}, u32[]{:S(2)}) collective-permute-start(f32[1,1,1,3,128]{4,3,0,2,1:T(4,128)S(1)} %copy.154), channel_id=1, source_target_pairs={{64,0},{128,64},{192,128},{256,192},{320,256},{384,320},{448,384},... | collective-permute-start | bytes 4616 | tf_op jit(solution)/shard_map/ppermute | solution.py:31
  16.1 15.0 %collective-permute-start.8 = (f32[4,1,1,128]{3,0,2,1:T(4,128)S(1)}, f32[4,1,1,128]{3,0,2,1:T(4,128)S(1)}, u32[]{:S(2)}, u32[]{:S(2)}) collective-permute-start(f32[4,1,1,128]{3,0,2,1:T(4,128)S(1)} %pad_maximum_fusion.13), channel_id=1, source_target_pairs={{0,16},{16,32},{32,48},{48,0},{1,17},{17,33},{33,49},{49,1},{2,18}... | collective-permute-start | bytes 6152 | tf_op jit(solution)/shard_map/ppermute | solution.py:29
  18.1 17.7 %collective-permute-start.9 = (f32[4,1,1,128]{3,0,2,1:T(4,128)S(1)}, f32[4,1,1,128]{3,0,2,1:T(4,128)S(1)}, u32[]{:S(2)}, u32[]{:S(2)}) collective-permute-start(f32[4,1,1,128]{3,0,2,1:T(4,128)S(1)} %pad_maximum_fusion.13), channel_id=1, source_target_pairs={{16,0},{32,16},{48,32},{0,48},{17,1},{33,17},{49,33},{1,49},{18,2}... | collective-permute-start | bytes 6152 | tf_op jit(solution)/shard_map/ppermute | solution.py:31
  22.7 15.0 %collective-permute-start.14 = (f32[4,1,1,3,128]{4,2,3,1,0:T(1,128)S(1)}, f32[4,1,1,3,128]{4,2,3,1,0:T(1,128)S(1)}, u32[]{:S(2)}, u32[]{:S(2)}) collective-permute-start(f32[4,1,1,3,128]{4,2,3,1,0:T(1,128)S(1)} %pad_maximum_fusion.10), channel_id=1, source_target_pairs={{0,16},{16,32},{32,48},{48,0},{1,17},{17,33},{33,49},{49,1},{2,18}... | collective-permute-start | bytes 18440 | tf_op jit(solution)/shard_map/ppermute | solution.py:29
  24.6 18.9 %collective-permute-start.15 = (f32[4,1,1,3,128]{4,2,3,1,0:T(1,128)S(1)}, f32[4,1,1,3,128]{4,2,3,1,0:T(1,128)S(1)}, u32[]{:S(2)}, u32[]{:S(2)}) collective-permute-start(f32[4,1,1,3,128]{4,2,3,1,0:T(1,128)S(1)} %pad_maximum_fusion.10), channel_id=1, source_target_pairs={{16,0},{32,16},{48,32},{0,48},{17,1},{33,17},{49,33},{1,49},{18,2}... | collective-permute-start | bytes 18440 | tf_op jit(solution)/shard_map/ppermute | solution.py:31
  29.2 16.3 %collective-permute-start.2 = (f32[4,1,1,3,128]{4,3,0,2,1:T(4,128)S(1)}, f32[4,1,1,3,128]{4,3,0,2,1:T(4,128)S(1)}, u32[]{:S(2)}, u32[]{:S(2)}) collective-permute-start(f32[4,1,1,3,128]{4,3,0,2,1:T(4,128)S(1)} %constant_dynamic-update-slice_fusion), channel_id=1, source_target_pairs={{0,16},{16,32},{32,48},{48,0},{1,17},{17,33},{33,49},{49,1},{2,18}... | collective-permute-start | bytes 18440 | tf_op jit(solution)/shard_map/ppermute | solution.py:29
  31.2 18.9 %collective-permute-start.3 = (f32[4,1,1,3,128]{4,3,0,2,1:T(4,128)S(1)}, f32[4,1,1,3,128]{4,3,0,2,1:T(4,128)S(1)}, u32[]{:S(2)}, u32[]{:S(2)}) collective-permute-start(f32[4,1,1,3,128]{4,3,0,2,1:T(4,128)S(1)} %constant_dynamic-update-slice_fusion), channel_id=1, source_target_pairs={{16,0},{32,16},{48,32},{0,48},{17,1},{33,17},{49,33},{1,49},{18,2}... | collective-permute-start | bytes 18440 | tf_op jit(solution)/shard_map/ppermute | solution.py:31
  35.8 16.3 %collective-permute-start.10 = (f32[4,3,1,128]{3,0,2,1:T(4,128)S(1)}, f32[4,3,1,128]{3,0,2,1:T(4,128)S(1)}, u32[]{:S(2)}, u32[]{:S(2)}) collective-permute-start(f32[4,3,1,128]{3,0,2,1:T(4,128)S(1)} %pad_maximum_fusion.9), channel_id=1, source_target_pairs={{0,1},{1,2},{2,3},{3,4},{4,5},{5,6},{6,7},{7,8},{8,9},{9,10},{10,1... | collective-permute-start | bytes 18440 | tf_op jit(solution)/shard_map/ppermute | solution.py:29
  37.7 18.9 %collective-permute-start.11 = (f32[4,3,1,128]{3,0,2,1:T(4,128)S(1)}, f32[4,3,1,128]{3,0,2,1:T(4,128)S(1)}, u32[]{:S(2)}, u32[]{:S(2)}) collective-permute-start(f32[4,3,1,128]{3,0,2,1:T(4,128)S(1)} %pad_maximum_fusion.9), channel_id=1, source_target_pairs={{1,0},{2,1},{3,2},{4,3},{5,4},{6,5},{7,6},{8,7},{9,8},{10,9},{11,1... | collective-permute-start | bytes 18440 | tf_op jit(solution)/shard_map/ppermute | solution.py:31
  43.6 13.1 %collective-permute-start.16 = (f32[4,3,1,3,128]{4,2,3,1,0:T(1,128)S(1)}, f32[4,3,1,3,128]{4,2,3,1,0:T(1,128)S(1)}, u32[]{:S(2)}, u32[]{:S(2)}) collective-permute-start(f32[4,3,1,3,128]{4,2,3,1,0:T(1,128)S(1)} %pad_maximum_fusion.6), channel_id=1, source_target_pairs={{0,1},{1,2},{2,3},{3,4},{4,5},{5,6},{6,7},{7,8},{8,9},{9,10},{10,1... | collective-permute-start | bytes 55304 | tf_op jit(solution)/shard_map/ppermute | solution.py:29
  45.5 11.2 %collective-permute-start.17 = (f32[4,3,1,3,128]{4,2,3,1,0:T(1,128)S(1)}, f32[4,3,1,3,128]{4,2,3,1,0:T(1,128)S(1)}, u32[]{:S(2)}, u32[]{:S(2)}) collective-permute-start(f32[4,3,1,3,128]{4,2,3,1,0:T(1,128)S(1)} %pad_maximum_fusion.6), channel_id=1, source_target_pairs={{1,0},{2,1},{3,2},{4,3},{5,4},{6,5},{7,6},{8,7},{9,8},{10,9},{11,1... | collective-permute-start | bytes 55304 | tf_op jit(solution)/shard_map/ppermute | solution.py:31
  50.1 6.6 collective-permute-start.4
  52.1 5.5 collective-permute-start.5
  176.3 6.8 collective-permute-start.18
  178.2 5.7 collective-permute-start.19
  184.0 6.5 collective-permute-start.20
  191.2 9.5 collective-permute-start.22
  416.4 6.8 collective-permute-start.26
  423.6 6.5 collective-permute-start.28
  550.9 6.5 collective-permute-start.30
  558.3 6.5 collective-permute-start.32
  565.6 6.9 collective-permute-start.34
  787.2 6.8 collective-permute-start.38
  794.5 6.5 collective-permute-start.40
  921.8 6.5 collective-permute-start.42
  929.2 6.8 collective-permute-start.44
  931.2 5.5 collective-permute-start.45
  936.7 6.2 collective-permute-start.46
  (21 other events, 80.7 us)
where the time goes:
time: 1060 us; the launch traced here: 1050 us
  blocking collectives  521 us (49%)
  loops' own time  224 us (21%)
  starting transfers between devices  141 us (13%)
  other arithmetic  111 us (10%)
  local copies, waits for them, and re-layouts  28.9 us (3%)
  waiting for transfers between devices  19.8 us (2%)
    psum x3, blocking collectives, squares(): return lax.psum(jnp.sum(vector * vector), ('gx', 'gy', 'gz'))  307 us
    another operation x3, loops' own time, shards(): lax.scan(visit_half, (own_field, jnp.zeros_like(padded_dip)), offsets)  224 us
    psum x2, blocking collectives, shards(): curve = lax.psum(jnp.sum(direction * applied), ('gx', 'gy', 'gz'))  214 us
    ppermute x18, starting transfers between devices, shifted(): return lax.ppermute(value, axis, pairs)  60.2 us
    ppermute x15, starting transfers between devices, extended(): lax.ppermute(head, axis, [((i + 1) % count, i) for i in range(count)])  53.9 us
    mul x39, other arithmetic, partner(): where_other = where_other + offset.astype(jnp.float32)[:, None] * CELL_EDGE  27.3 us
    add x39, other arithmetic, partner(): corner = offset + 1  27.3 us
    ppermute x15, starting transfers between devices, extended(): lax.ppermute(tail, axis, [(i, (i + 1) % count) for i in range(count)])  26.5 us
  transfers between devices with their start and end apart: 48, of which 21 were waited for; matrix products, arithmetic and copies ran while one was open for 0% of the time, Pallas kernels for 0%

commit v1 on v0

v1 whole, which is shorter than its diff:
```python
import functools
import math

import jax
import jax.numpy as jnp
from jax import lax
from jax.experimental import pallas as pl
from jax.experimental.pallas import tpu as pltpu
from jax.sharding import PartitionSpec as P

CL = 128
CELL_EDGE = 11.0
CUTOFF = 9.0
THOLE_A = 0.39
SHIFT = 1.5
AXES = ("gx", "gy", "gz")
MESH = pl.DeviceIdType.MESH
ROWS = 32
BLOCKS = CL // ROWS
HOMES = 2
SELF = 13
UNIT = 1.0 / CUTOFF
LN2 = math.log(2.0)
TOTAL = 3.0 * UNIT**3
F32 = jnp.float32

OFFSETS = sorted(
    [
        (ex, ey, ez)
        for ex in (-1, 0, 1)
        for ey in (-1, 0, 1)
        for ez in (-1, 0, 1)
        if (ex, ey, ez) != (0, 0, 0)
    ],
    key=lambda o: -sum(abs(e) for e in o),
)


def stages(sizes):
    first = [(i, j, 0) for i in range(sizes[0]) for j in range(sizes[1]) if (i, j) != (0, 0)]
    second = [(0, 0, k) for k in range(1, sizes[2])]
    return (first, second)


def kernel(
    sizes,
    pos_ref,
    pol_ref,
    perm_ref,
    grp_ref,
    occ_ref,
    dip_ref,
    res_ref,
    halo,
    halo_v,
    staged,
    home,
    tens,
    acc,
    basis,
    red_a,
    red_b,
    halo_send,
    halo_recv,
    red_send_a,
    red_recv_a,
    red_send_b,
    red_recv_b,
):
    here = tuple(lax.axis_index(a) for a in AXES)
    groups_of = stages(sizes)

    def device(offset):
        return tuple(
            lax.rem(h + (o + n) % n, n) if o else h for h, o, n in zip(here, offset, sizes)
        )

    peers = {tuple((e + n) % n for e, n in zip(o, sizes)) for o in OFFSETS}
    for stage in groups_of:
        peers |= set(stage)
    barrier = pltpu.get_barrier_semaphore()
    for o in sorted(peers):
        pl.semaphore_signal(barrier, inc=1, device_id=device(o), device_id_type=MESH)

    lane = lax.broadcasted_iota(jnp.int32, (1, CL), 1)
    eye = lax.broadcasted_iota(jnp.int32, (CL, CL), 0) == lax.broadcasted_iota(
        jnp.int32, (CL, CL), 1
    )

    live = []
    invpol = []
    for h in range(HOMES):
        alive = (lane < occ_ref[h, 0, 0]).astype(F32)
        live.append(alive)
        pol = pol_ref[h, 0, :, :]
        inv = 1.0 / pol
        invpol.append(inv)
        q = lax.rsqrt(pol)
        mat = jnp.concatenate(
            [
                pos_ref[h, 0, 0] * UNIT,
                q,
                alive * perm_ref[h, 0, 0],
                grp_ref[h, 0, :, :].astype(F32),
            ],
            axis=0,
        )
        halo[1 + h, 4] = mat
        for a in range(3):
            basis[0, h, a] = mat[4 + a : 5 + a]
        cols = jnp.transpose(mat)
        for slot, k in enumerate((0, 1, 2, 3, 7)):
            home[h, slot] = jnp.broadcast_to(cols[:, k : k + 1], (CL, CL))

    pl.semaphore_wait(barrier, len(peers))

    def exchange(buf, k):
        copies = []
        for s, (ex, ey, ez) in enumerate(OFFSETS):
            source, target = 4, (1 - ey) * 3 + (1 - ez)
            if ex == 0:
                src, dst = buf.at[pl.ds(1, 2), source], buf.at[pl.ds(1, 2), target]
            elif ex == 1:
                src, dst = buf.at[2, source], buf.at[0, target]
            else:
                src, dst = buf.at[1, source], buf.at[3, target]
            copies.append(
                pltpu.make_async_remote_copy(
                    src_ref=src,
                    dst_ref=dst,
                    send_sem=halo_send.at[k, s],
                    recv_sem=halo_recv.at[k, s],
                    device_id=device((ex, ey, ez)),
                    device_id_type=MESH,
                )
            )
        for c in copies:
            c.start()
        return copies

    def shifted(x, yz):
        offset = ((x - 1) * CELL_EDGE, (yz // 3 - 1) * CELL_EDGE, (yz % 3 - 1) * CELL_EDGE)
        sub = lax.broadcasted_iota(jnp.int32, (8, CL), 0)
        add = jnp.zeros((8, CL), F32)
        for a in range(3):
            if offset[a]:
                add = jnp.where(sub == a, jnp.float32(offset[a] * UNIT), add)
        staged[x * 9 + yz] = halo[x, yz] + add

    def block_rows(i):
        return pl.ds(pl.multiple_of(i * ROWS, ROWS), ROWS)

    def couple(it, h, i, n, cell, total, own):
        rows = block_rows(i)
        r = [staged[cell, a : a + 1, :] - home[h, a, rows, :] for a in range(3)]
        d2 = r[0] * r[0] + r[1] * r[1] + r[2] * r[2]
        if own:
            diagonal = lax.broadcasted_iota(jnp.int32, (ROWS, CL), 0) + i * ROWS
            diagonal = diagonal == lax.broadcasted_iota(jnp.int32, (ROWS, CL), 1)
            d2 = d2 + diagonal.astype(F32)
        inv = lax.rsqrt(d2)
        inv2 = inv * inv
        taper = jnp.maximum(1.0 - d2, 0.0)
        g = (taper * taper) * (inv2 * inv)
        if own:
            g = jnp.where(staged[cell, 7:8, :] != home[h, 4, rows, :], g, 0.0)
        t = (d2 * d2 * inv) * (home[h, 3, rows, :] * staged[cell, 3:4, :])
        falloff = jnp.exp2(t)
        ge = g * falloff
        c3 = g - ge
        c5 = (c3 + (LN2 * t) * ge) * inv2
        c3 = c3 * (1.0 / 3.0)
        p = [c5 * r[a] for a in range(3)]
        xx = p[0] * r[0] - c3
        yy = p[1] * r[1] - c3
        zz = p[2] * r[2] - c3
        xy = p[0] * r[1]
        xz = p[0] * r[2]
        yz = p[1] * r[2]
        for c, m in enumerate((xx, yy, zz, xy, xz, yz)):
            tens[it, n, c] = m
        v = [staged[cell, 4 + a : 5 + a, :] for a in range(3)]
        return product((xx, yy, zz, xy, xz, yz), v, total)

    def product(m, v, total):
        xx, yy, zz, xy, xz, yz = m
        out = (
            xx * v[0] + xy * v[1] + xz * v[2],
            xy * v[0] + yy * v[1] + yz * v[2],
            xz * v[0] + yz * v[1] + zz * v[2],
        )
        if total is None:
            return out
        return tuple(t + o for t, o in zip(total, out))

    def apply(it, n, v, total):
        return product([tens[it, n, c] for c in range(6)], v, total)

    for h in range(HOMES):
        if h:
            home[h, 0] = home[h, 0] + CELL_EDGE * UNIT * h
        home[h, 3] = home[h, 3] * (-THOLE_A / LN2 / UNIT**3)

    common = [n for n in range(27) if n not in (4, SELF, 22)]

    def inner_first(it, unused):
        h, i = it // BLOCKS, it % BLOCKS
        total = couple(it, h, i, SELF, h * 9 + SELF, None, True)
        total = couple(it, h, i, 22 - 18 * h, (2 - h) * 9 + 4, total, False)
        for a in range(3):
            acc[it, a] = total[a]
        return unused

    def outer_first(it, unused):
        h, i = it // BLOCKS, it % BLOCKS
        total = tuple(acc[it, a] for a in range(3))
        for n in common:
            total = couple(it, h, i, n, h * 9 + n, total, False)
        total = couple(it, h, i, 4 + 18 * h, 27 * h + 4, total, False)
        for a in range(3):
            acc[it, a] = total[a]
        return unused

    def inner_later(k, it, unused):
        h = it // BLOCKS
        total = None
        for n, x in ((SELF, 1 + h), (22 - 18 * h, 2 - h)):
            total = apply(it, n, [halo_v[k, x, 4, a] for a in range(3)], total)
        for a in range(3):
            acc[it, a] = total[a]
        return unused

    def outer_later(k, it, unused):
        h = it // BLOCKS
        total = tuple(acc[it, a] for a in range(3))
        for n in common:
            total = apply(it, n, [halo_v[k, h + n // 9, n % 9, a] for a in range(3)], total)
        total = apply(it, 4 + 18 * h, [halo_v[k, 3 * h, 4, a] for a in range(3)], total)
        for a in range(3):
            acc[it, a] = total[a]
        return unused

    def image(k):
        for h in range(HOMES):
            for a in range(3):
                field = jnp.concatenate([acc[h * BLOCKS + i, a] for i in range(BLOCKS)], axis=0)
                column = jnp.sum(field, axis=1, keepdims=True)
                row = jnp.sum(jnp.where(eye, column, 0.0), axis=0, keepdims=True)
                v = basis[k, h, a]
                nxt = live[h] * (v * invpol[h] - TOTAL * row) - SHIFT * v
                basis[k + 1, h, a] = nxt
                if k < 2:
                    halo_v[k, 1 + h, 4, a] = nxt

    pending = exchange(halo, 0)
    shifted(1, 4)
    shifted(2, 4)
    lax.fori_loop(0, HOMES * BLOCKS, inner_first, 0)
    for c in pending:
        c.wait_recv()
    for x in range(4):
        for yz in range(9):
            if not (yz == 4 and x in (1, 2)):
                shifted(x, yz)
    lax.fori_loop(0, HOMES * BLOCKS, outer_first, 0)
    image(0)
    started = list(pending)
    for k in range(2):
        pending = exchange(halo_v.at[k], 1 + k)
        started += pending
        lax.fori_loop(0, HOMES * BLOCKS, functools.partial(inner_later, k), 0)
        for c in pending:
            c.wait_recv()
        lax.fori_loop(0, HOMES * BLOCKS, functools.partial(outer_later, k), 0)
        image(1 + k)

    row = jnp.zeros((1, CL), F32)
    for m in range(6):
        part = jnp.zeros((1, CL), F32)
        for h in range(HOMES):
            for a in range(3):
                part = part + basis[m // 2, h, a] * basis[(m + 1) // 2, h, a]
        row = jnp.where(lane == m, jnp.sum(part, axis=1, keepdims=True), row)

    for stage, buf, send, recv in (
        (groups_of[0], red_a, red_send_a, red_recv_a),
        (groups_of[1], red_b, red_send_b, red_recv_b),
    ):
        buf[0] = row
        pending = [
            pltpu.make_async_remote_copy(
                src_ref=buf.at[0],
                dst_ref=buf.at[1 + s],
                send_sem=send.at[s],
                recv_sem=recv.at[s],
                device_id=device(o),
                device_id_type=MESH,
            )
            for s, o in enumerate(stage)
        ]
        for c in pending:
            c.start()
        started += pending
        for c in pending:
            c.wait_recv()
        parts = [buf[s] for s in range(1 + len(stage))]
        while len(parts) > 1:
            parts = [
                parts[s] + parts[s + 1] if s + 1 < len(parts) else parts[s]
                for s in range(0, len(parts), 2)
            ]
        row = parts[0]

    moment = [
        jnp.sum(jnp.where(lane == m, row, 0.0), axis=1, keepdims=True) for m in range(6)
    ]

    def dot(left, right):
        total = None
        for i, x in enumerate(left):
            for j, y in enumerate(right):
                term = moment[i + j] * (x * y)
                total = term if total is None else total + term
        return total

    one = jnp.ones((1, 1), F32)
    res, direction, dip = [one], [one], []
    norm = moment[0]
    for iteration in range(3):
        applied = [SHIFT * c for c in direction] + [jnp.zeros((1, 1), F32)]
        applied = [
            c if i == 0 else c + direction[i - 1] for i, c in enumerate(applied)
        ]
        step = norm / dot(direction, applied)
        dip = [
            step * c + (dip[i] if i < len(dip) else 0.0) for i, c in enumerate(direction)
        ]
        res = [
            (res[i] if i < len(res) else 0.0) - step * c for i, c in enumerate(applied)
        ]
        if iteration < 2:
            new = dot(res, res)
            ratio = new / norm
            direction = [
                c + (ratio * direction[i] if i < len(direction) else 0.0)
                for i, c in enumerate(res)
            ]
            norm = new
    for h in range(HOMES):
        for a in range(3):
            v = [basis[k, h, a] for k in range(4)]
            dip_ref[h, 0, 0, a : a + 1, :] = dip[0] * v[0] + dip[1] * v[1] + dip[2] * v[2]
            res_ref[h, 0, 0, a : a + 1, :] = (
                res[0] * v[0] + res[1] * v[1] + res[2] * v[2] + res[3] * v[3]
            )
    for c in started:
        c.wait_send()


def solution(mesh):
    sizes = tuple(mesh.shape[a] for a in AXES)
    first, second = stages(sizes)
    vector = jax.ShapeDtypeStruct((HOMES, 1, 1, 3, CL), F32)
    vmem = pl.BlockSpec(memory_space=pltpu.VMEM)
    call = pl.pallas_call(
        functools.partial(kernel, sizes),
        out_shape=(vector, vector),
        in_specs=[vmem] * 4 + [pl.BlockSpec(memory_space=pltpu.SMEM)],
        out_specs=(vmem, vmem),
        scratch_shapes=[
            pltpu.VMEM((4, 9, 8, CL), F32),
            pltpu.VMEM((2, 4, 9, 3, 1, CL), F32),
            pltpu.VMEM((36, 8, CL), F32),
            pltpu.VMEM((HOMES, 5, CL, CL), F32),
            pltpu.VMEM((HOMES * BLOCKS, 27, 6, ROWS, CL), F32),
            pltpu.VMEM((HOMES * BLOCKS, 3, ROWS, CL), F32),
            pltpu.VMEM((4, HOMES, 3, 1, CL), F32),
            pltpu.VMEM((1 + len(first), 1, CL), F32),
            pltpu.VMEM((1 + len(second), 1, CL), F32),
            pltpu.SemaphoreType.DMA((3, 26)),
            pltpu.SemaphoreType.DMA((3, 26)),
            pltpu.SemaphoreType.DMA((len(first),)),
            pltpu.SemaphoreType.DMA((len(first),)),
            pltpu.SemaphoreType.DMA((len(second),)),
            pltpu.SemaphoreType.DMA((len(second),)),
        ],
        compiler_params=pltpu.CompilerParams(
            collective_id=0, has_side_effects=True, vmem_limit_bytes=48 * 1024 * 1024
        ),
    )
    return jax.shard_map(
        call,
        mesh=mesh,
        in_specs=(
            P("gx", "gy", "gz", None, None),
            P("gx", "gy", "gz", None),
            P("gx", "gy", "gz", None, None),
            P("gx", "gy", "gz", None),
            P("gx", "gy", "gz"),
        ),
        out_specs=(P("gx", "gy", "gz", None, None), P("gx", "gy", "gz", None, None)),
        check_vma=False,
    )
```

time: 1060 us -> 64.3 us (0.06)
  blocking collectives: 521 us -> 0 us
  loops' own time: 224 us -> 0 us
  starting transfers between devices: 141 us -> 0 us
  other arithmetic: 111 us -> 0 us
  Pallas kernels: 0 us -> 60.2 us
  local copies, waits for them, and re-layouts: 28.9 us -> 3.3 us
  waiting for transfers between devices: 19.8 us -> 0 us
    psum x5 -> x0, blocking collectives: 521 us -> none  [the longest x3 307 us: squares(): return lax.psum(jnp.sum(vector * vector), ('gx', 'gy', 'gz'))]
    another operation x3 -> x0, loops' own time: 224 us -> none  [shards(): lax.scan(visit_half, (own_field, jnp.zeros_like(padded_dip)), offsets)]
    ppermute x48 -> x0, starting transfers between devices: 141 us -> none  [the longest x18 60.2 us: shifted(): return lax.ppermute(value, axis, pairs)]
    pallas_call x0 -> x1, Pallas kernels: none -> 60.2 us
    reduce_sum x129 -> x0, other arithmetic: 40.1 us -> none  [the longest x39 15.9 us: field_other(): project = jnp.sum(separation * source_home[..., :, :, None], axis=-3)]
    mul x122 -> x0, other arithmetic: 38.5 us -> none  [the longest x39 27.3 us: partner(): where_other = where_other + offset.astype(jnp.float32)[:, None] * CELL_EDGE]
    add x50 -> x0, other arithmetic: 27.4 us -> none  [the longest x39 27.3 us: partner(): corner = offset + 1]
    slice x47 -> x0, local copies, waits for them, and re-layouts: 25.9 us -> none  [the longest x39 25.9 us: partner(): start_five = (corner[0], corner[1], corner[2], zero_index, zero_index)]
  transfers between devices with their start and end apart: 48 -> 0, of which waited for: 21 -> 0; matrix products, arithmetic and copies ran while one was open for 0% -> 0% of each run, Pallas kernels for 0% -> 0%
where the time goes in v1:
time: 64.3 us; the launch traced here: 64.1 us
  Pallas kernels  60.2 us (94%)
  local copies, waits for them, and re-layouts  3.3 us (5%)
  between operations  0.65 us (1%)
    pallas_call x1, Pallas kernels  60.2 us
    unnamed x9, local copies, waits for them, and re-layouts  2.13 us

profile of v1, /device:TPU:1, one launch (start us, length us, event | category | flops | bytes accessed | tf_op | source)
XLA Modules:
  0.0 64.1 jit_solution(11955927134980939712)
XLA Ops:
  0.6 0.7 %copy.9.occ_ref = s32[2,1,1]{2,1,0:T(1,128)S(1)} copy(s32[2,1,1]{0,2,1:T(1,128)} %param.9) | data formatting | bytes 16 | tf_op args[4]
  1.4 0.0 copy-start.2
  1.4 0.7 %copy.7.pos_ref = f32[2,1,1,3,128]{4,3,2,1,0:T(4,128)S(1)} copy(f32[2,1,1,3,128]{4,2,3,1,0:T(1,128)} %param.5) | data formatting | bytes 6144 | tf_op args[0]
  2.1 0.0 copy-done.2
  2.1 0.0 copy-start
  2.1 0.0 copy-start.1
  2.1 0.7 %copy-done = f32[2,1,1,128]{3,2,1,0:T(1,128)S(1)} copy-done((f32[2,1,1,128]{3,2,1,0:T(1,128)S(1)}, f32[2,1,1,128]{3,2,1,0:T(1,128)}, u32[]{:S(2)}) %copy-start) | copy-done | bytes 1048
  2.8 0.0 copy-done.1
  2.8 60.2 %shard_map.68 = (f32[2,1,1,3,128]{4,3,2,1,0:T(4,128)S(1)}, f32[2,1,1,3,128]{4,3,2,1,0:T(4,128)S(1)}) custom-call(f32[2,1,1,3,128]{4,3,2,1,0:T(4,128)S(1)} %copy.7.pos_ref, f32[2,1,1,128]{3,2,1,0:T(1,128)S(1)} %copy-done, f32[2,1,1,3,128]{4,3,2,1,0:T(4,128)S(1)} %copy.8.perm_ref, s32[2,1,1,128]{3,2,1,0:T(1,128)S(1)} %copy-done.1, s32[2,1,1]{2,1,0:T(1,128)S(1)} %copy.9.occ_ref), custom_call_target="tpu_custom_call" | custom-call | tf_op jit(solution)/shard_map/pallas_call
  62.9 0.6 copy.10
  63.5 0.6 copy.11
  (1 shorter events, 0.0 us)
Async XLA Ops:
  1.4 0.7 %copy-start.2 = (f32[2,1,1,3,128]{4,2,3,1,0:T(1,128)S(1)}, f32[2,1,1,3,128]{4,2,3,1,0:T(1,128)}, u32[]{:S(2)}) copy-start(f32[2,1,1,3,128]{4,2,3,1,0:T(1,128)} %param.7) | copy-start | bytes 9220
  2.1 0.7 %copy-start = (f32[2,1,1,128]{3,2,1,0:T(1,128)S(1)}, f32[2,1,1,128]{3,2,1,0:T(1,128)}, u32[]{:S(2)}) copy-start(f32[2,1,1,128]{3,2,1,0:T(1,128)} %pol_ref.1) | copy-start | bytes 3076
  2.1 0.7 %copy-start.1 = (s32[2,1,1,128]{3,2,1,0:T(1,128)S(1)}, s32[2,1,1,128]{3,2,1,0:T(1,128)}, u32[]{:S(2)}) copy-start(s32[2,1,1,128]{3,2,1,0:T(1,128)} %grp_ref.1) | copy-start | bytes 3076

commit v2 on v1

v2 whole, which is shorter than its diff:
```python
import functools
import math

import jax
import jax.numpy as jnp
from jax import lax
from jax.experimental import pallas as pl
from jax.experimental.pallas import tpu as pltpu
from jax.sharding import PartitionSpec as P

CL = 128
CELL_EDGE = 11.0
CUTOFF = 9.0
THOLE_A = 0.39
SHIFT = 1.5
AXES = ("gx", "gy", "gz")
MESH = pl.DeviceIdType.MESH
HOMES = 2
ROWS = 32
BLOCKS = CL // ROWS
TALL = 64
TALLS = CL // TALL
UNIT = 1.0 / CUTOFF
LN2 = math.log(2.0)
TOTAL = 3.0 * UNIT**3
F32 = jnp.float32

FACES = ((-1, 0), (1, 0), (0, -1), (0, 1))
EDGES = ((-1, -1), (-1, 1), (1, -1), (1, 1))

GROUPS = ((2, 10), (12, 16), (28, 8))


def slot_of(dx, dy, dz):
    if dx == 0:
        return 2 + 2 * FACES.index((dy, dz)) if (dy, dz) in FACES else 12 + 2 * EDGES.index((dy, dz))
    side = 0 if dx < 0 else 1
    if (dy, dz) == (0, 0):
        return 10 + side
    if (dy, dz) in FACES:
        return 20 + 4 * side + FACES.index((dy, dz))
    return 28 + 4 * side + EDGES.index((dy, dz))


OFFSETS = sorted(
    [
        (ex, ey, ez)
        for ex in (-1, 0, 1)
        for ey in (-1, 0, 1)
        for ez in (-1, 0, 1)
        if (ex, ey, ez) != (0, 0, 0)
    ],
    key=lambda o: -sum(abs(e) for e in o),
)


def places():
    where = {0: (0, 0, 0), 1: (1, 0, 0)}
    for dx, dy, dz in OFFSETS:
        first = slot_of(dx, dy, dz)
        if dx == 0:
            where[first], where[first + 1] = (0, dy, dz), (1, dy, dz)
        else:
            where[first] = (-1 if dx < 0 else 2, dy, dz)
    return where


PLACES = places()


def stages(sizes):
    first = [(i, j, 0) for i in range(sizes[0]) for j in range(sizes[1]) if (i, j) != (0, 0)]
    second = [(0, 0, k) for k in range(1, sizes[2])]
    return (first, second)


def kernel(
    sizes,
    pos_ref,
    pol_ref,
    perm_ref,
    grp_ref,
    occ_ref,
    dip_ref,
    res_ref,
    inbox,
    inbox_grp,
    inbox_occ,
    halo,
    halo_v,
    staged,
    home,
    tens,
    acc,
    basis,
    red_a,
    red_b,
    in_sem,
    halo_send,
    halo_recv,
    red_send,
    red_recv,
):
    fetches = [
        pltpu.make_async_copy(pos_ref, inbox.at[pl.ds(0, 6)], in_sem.at[0]),
        pltpu.make_async_copy(perm_ref, inbox.at[pl.ds(6, 6)], in_sem.at[1]),
        pltpu.make_async_copy(pol_ref, inbox.at[pl.ds(12, 2)], in_sem.at[2]),
        pltpu.make_async_copy(grp_ref, inbox_grp, in_sem.at[3]),
        pltpu.make_async_copy(occ_ref, inbox_occ, in_sem.at[4]),
    ]
    for c in fetches:
        c.start()

    here = tuple(lax.axis_index(a) for a in AXES)
    near = [
        {
            o: h if o == 0 else lax.rem(h + (o + n), n)
            for o in (-1, 0, 1)
        }
        for h, n in zip(here, sizes)
    ]

    def device(offset):
        return tuple(
            near[d][o] if o in near[d] else lax.rem(here[d] + o, sizes[d])
            for d, o in enumerate(offset)
        )

    groups_of = stages(sizes)

    def wrapped(o):
        return tuple((e + n) % n for e, n in zip(o, sizes))

    peers = list(OFFSETS)
    known = {wrapped(o) for o in OFFSETS}
    for stage in groups_of:
        peers += [o for o in stage if o not in known]
    barrier = pltpu.get_barrier_semaphore()
    for o in peers:
        pl.semaphore_signal(barrier, inc=1, device_id=device(o), device_id_type=MESH)

    lane = lax.broadcasted_iota(jnp.int32, (1, CL), 1)
    eye = lax.broadcasted_iota(jnp.int32, (CL, CL), 0) == lax.broadcasted_iota(
        jnp.int32, (CL, CL), 1
    )

    for c in fetches:
        c.wait()
    live = []
    invpol = []
    for h in range(HOMES):
        alive = (lane < inbox_occ[h]).astype(F32)
        live.append(alive)
        pol = inbox[12 + h]
        invpol.append(1.0 / pol)
        for a in range(3):
            halo[h, a : a + 1, :] = inbox[3 * h + a] * UNIT
            vector = alive * inbox[6 + 3 * h + a]
            halo[h, 4 + a : 5 + a, :] = vector
            basis[0, h, a] = vector
        halo[h, 3:4, :] = lax.rsqrt(pol)
        halo[h, 7:8, :] = inbox_grp[h].astype(F32)

    pl.semaphore_wait(barrier, len(peers))

    def exchange(buf, k):
        for ex, ey, ez in OFFSETS:
            target = slot_of(-ex, -ey, -ez)
            if ex == 0:
                src, dst = buf.at[pl.ds(0, 2)], buf.at[pl.ds(target, 2)]
            else:
                source = 1 if ex == 1 else 0
                src, dst = buf.at[pl.ds(source, 1)], buf.at[pl.ds(target, 1)]
            group = sum(abs(e) for e in (ex, ey, ez)) - 1
            pltpu.make_async_remote_copy(
                src_ref=src,
                dst_ref=dst,
                send_sem=halo_send.at[k],
                recv_sem=halo_recv.at[k, group],
                device_id=device((ex, ey, ez)),
                device_id_type=MESH,
            ).start()

    def arrived(buf, k, group):
        region = buf.at[pl.ds(*GROUPS[group])]
        pltpu.make_async_copy(region, region, halo_recv.at[k, group]).wait()

    def sent(buf, k):
        region = buf.at[pl.ds(2, 34)]
        pltpu.make_async_copy(region, region, halo_send.at[k]).wait()

    def place(slot):
        sub = lax.broadcasted_iota(jnp.int32, (8, CL), 0)
        add = jnp.zeros((8, CL), F32)
        for a in range(3):
            if PLACES[slot][a]:
                add = jnp.where(sub == a, jnp.float32(PLACES[slot][a] * CELL_EDGE * UNIT), add)
        staged[slot] = halo[slot] + add

    def couple(h, i, n, slot, total, own):
        rows = pl.ds(pl.multiple_of(i * ROWS, ROWS), ROWS)
        r = [staged[slot, a : a + 1, :] - home[h, a, rows, :] for a in range(3)]
        d2 = r[0] * r[0] + r[1] * r[1] + r[2] * r[2]
        if own:
            diagonal = lax.broadcasted_iota(jnp.int32, (ROWS, CL), 0) + i * ROWS
            diagonal = diagonal == lax.broadcasted_iota(jnp.int32, (ROWS, CL), 1)
            d2 = d2 + diagonal.astype(F32)
        inv = lax.rsqrt(d2)
        inv2 = inv * inv
        taper = jnp.maximum(1.0 - d2, 0.0)
        g = (taper * taper) * (inv2 * inv)
        if own:
            g = jnp.where(staged[slot, 7:8, :] != home[h, 4, rows, :], g, 0.0)
        t = (d2 * d2 * inv) * (home[h, 3, rows, :] * staged[slot, 3:4, :])
        falloff = jnp.exp2(t)
        ge = g * falloff
        c3 = g - ge
        c5 = (c3 + (LN2 * t) * ge) * inv2
        c3 = c3 * (1.0 / 3.0)
        p = [c5 * r[a] for a in range(3)]
        m = (
            p[0] * r[0] - c3,
            p[1] * r[1] - c3,
            p[2] * r[2] - c3,
            p[0] * r[1],
            p[0] * r[2],
            p[1] * r[2],
        )
        for c in range(6):
            tens[h, n, c, rows, :] = m[c]
        return product(m, [staged[slot, 4 + a : 5 + a, :] for a in range(3)], total)

    def product(m, v, total):
        xx, yy, zz, xy, xz, yz = m
        out = (
            xx * v[0] + xy * v[1] + xz * v[2],
            xy * v[0] + yy * v[1] + yz * v[2],
            xz * v[0] + yz * v[1] + zz * v[2],
        )
        if total is None:
            return out
        return tuple(t + o for t, o in zip(total, out))

    def members(group, h):
        if group == 0:
            return [(n, 2 + n - 2) for n in range(2, 10)] + [(10, 10 + h)]
        if group == 1:
            return [(11 + n, 12 + n) for n in range(8)] + [(19 + n, 20 + 4 * h + n) for n in range(4)]
        return [(23 + n, 28 + 4 * h + n) for n in range(4)]

    def first_own(it, unused):
        h, i = it // BLOCKS, it % BLOCKS
        total = couple(h, i, 0, h, None, True)
        total = couple(h, i, 1, 1 - h, total, False)
        rows = pl.ds(pl.multiple_of(i * ROWS, ROWS), ROWS)
        for a in range(3):
            acc[h, a, rows, :] = total[a]
        return unused

    def first_group(group, it, unused):
        h, i = it // BLOCKS, it % BLOCKS
        rows = pl.ds(pl.multiple_of(i * ROWS, ROWS), ROWS)
        total = tuple(acc[h, a, rows, :] for a in range(3))
        for n, slot in members(group, h):
            total = couple(h, i, n, slot, total, False)
        for a in range(3):
            acc[h, a, rows, :] = total[a]
        return unused

    def apply(k, h, rows, n, slot, total):
        return product(
            [tens[h, n, c, rows, :] for c in range(6)], [halo_v[k, slot, a] for a in range(3)], total
        )

    def later_own(k, it, unused):
        h, i = it // TALLS, it % TALLS
        rows = pl.ds(pl.multiple_of(i * TALL, TALL), TALL)
        total = apply(k, h, rows, 0, h, None)
        total = apply(k, h, rows, 1, 1 - h, total)
        for a in range(3):
            acc[h, a, rows, :] = total[a]
        return unused

    def later_group(k, group, it, unused):
        h, i = it // TALLS, it % TALLS
        rows = pl.ds(pl.multiple_of(i * TALL, TALL), TALL)
        total = tuple(acc[h, a, rows, :] for a in range(3))
        shared = (8, 8, 0)[group]
        rim, slot = ((10, 10 + h), (19, 20 + 4 * h), (23, 28 + 4 * h))[group]
        base = (2, 11, 0)[group]
        if shared:
            total = lax.fori_loop(
                0,
                shared,
                lambda c, t: apply(k, h, rows, base + c, GROUPS[group][0] + c, t),
                total,
            )
        if group == 0:
            total = apply(k, h, rows, rim, slot, total)
        else:
            total = lax.fori_loop(
                0, 4, lambda c, t: apply(k, h, rows, rim + c, slot + c, t), total
            )
        for a in range(3):
            acc[h, a, rows, :] = total[a]
        return unused

    def image(k):
        for h in range(HOMES):
            for a in range(3):
                column = jnp.sum(acc[h, a], axis=1, keepdims=True)
                row = jnp.sum(jnp.where(eye, column, 0.0), axis=0, keepdims=True)
                v = basis[k, h, a]
                nxt = live[h] * (v * invpol[h] - TOTAL * row) - SHIFT * v
                basis[k + 1, h, a] = nxt
                if k < 2:
                    halo_v[k, h, a] = nxt

    exchange(halo, 0)
    for h in range(HOMES):
        place(h)
        cols = jnp.transpose(staged[h])
        for entry, c in enumerate((0, 1, 2, 3, 7)):
            col = cols[:, c : c + 1]
            if c == 3:
                col = col * (-THOLE_A / LN2 / UNIT**3)
            home[h, entry] = jnp.broadcast_to(col, (CL, CL))
    lax.fori_loop(0, HOMES * BLOCKS, first_own, 0)
    for group in range(3):
        arrived(halo, 0, group)
        for slot in range(GROUPS[group][0], sum(GROUPS[group])):
            place(slot)
        lax.fori_loop(0, HOMES * BLOCKS, functools.partial(first_group, group), 0)
    image(0)
    for k in range(2):
        exchange(halo_v.at[k], 1 + k)
        lax.fori_loop(0, HOMES * TALLS, functools.partial(later_own, k), 0)
        for group in range(3):
            arrived(halo_v.at[k], 1 + k, group)
            lax.fori_loop(0, HOMES * TALLS, functools.partial(later_group, k, group), 0)
        image(1 + k)

    row = jnp.zeros((1, CL), F32)
    for m in range(6):
        part = jnp.zeros((1, CL), F32)
        for h in range(HOMES):
            for a in range(3):
                part = part + basis[m // 2, h, a] * basis[(m + 1) // 2, h, a]
        row = jnp.where(lane == m, jnp.sum(part, axis=1, keepdims=True), row)

    for s, (stage, buf) in enumerate(zip(groups_of, (red_a, red_b))):
        buf[0] = row
        for i, o in enumerate(stage):
            pltpu.make_async_remote_copy(
                src_ref=buf.at[0],
                dst_ref=buf.at[1 + i],
                send_sem=red_send.at[s],
                recv_sem=red_recv.at[s],
                device_id=device(o),
                device_id_type=MESH,
            ).start()
        region = buf.at[pl.ds(1, len(stage))]
        pltpu.make_async_copy(region, region, red_recv.at[s]).wait()
        parts = [buf[i] for i in range(1 + len(stage))]
        while len(parts) > 1:
            parts = [
                parts[i] + parts[i + 1] if i + 1 < len(parts) else parts[i]
                for i in range(0, len(parts), 2)
            ]
        row = parts[0]

    moment = [
        jnp.sum(jnp.where(lane == m, row, 0.0), axis=1, keepdims=True) for m in range(6)
    ]

    def dot(left, right):
        total = None
        for i, x in enumerate(left):
            for j, y in enumerate(right):
                term = moment[i + j] * (x * y)
                total = term if total is None else total + term
        return total

    one = jnp.ones((1, 1), F32)
    res, direction, dip = [one], [one], []
    norm = moment[0]
    for iteration in range(3):
        applied = [SHIFT * c for c in direction] + [jnp.zeros((1, 1), F32)]
        applied = [
            c if i == 0 else c + direction[i - 1] for i, c in enumerate(applied)
        ]
        step = norm / dot(direction, applied)
        dip = [
            step * c + (dip[i] if i < len(dip) else 0.0) for i, c in enumerate(direction)
        ]
        res = [
            (res[i] if i < len(res) else 0.0) - step * c for i, c in enumerate(applied)
        ]
        if iteration < 2:
            new = dot(res, res)
            ratio = new / norm
            direction = [
                c + (ratio * direction[i] if i < len(direction) else 0.0)
                for i, c in enumerate(res)
            ]
            norm = new
    for h in range(HOMES):
        for a in range(3):
            v = [basis[k, h, a] for k in range(4)]
            dip_ref[3 * h + a] = dip[0] * v[0] + dip[1] * v[1] + dip[2] * v[2]
            res_ref[3 * h + a] = res[0] * v[0] + res[1] * v[1] + res[2] * v[2] + res[3] * v[3]
    sent(halo, 0)
    for k in range(2):
        sent(halo_v.at[k], 1 + k)
    for s, (stage, buf) in enumerate(zip(groups_of, (red_a, red_b))):
        region = buf.at[pl.ds(1, len(stage))]
        pltpu.make_async_copy(region, region, red_send.at[s]).wait()


def solution(mesh):
    sizes = tuple(mesh.shape[a] for a in AXES)
    first, second = stages(sizes)
    vector = jax.ShapeDtypeStruct((HOMES * 3, 1, CL), F32)
    vmem = pl.BlockSpec(memory_space=pltpu.VMEM)
    call = pl.pallas_call(
        functools.partial(kernel, sizes),
        out_shape=(vector, vector),
        in_specs=[pl.BlockSpec(memory_space=pl.ANY)] * 5,
        out_specs=(vmem, vmem),
        scratch_shapes=[
            pltpu.VMEM((14, 1, CL), F32),
            pltpu.VMEM((HOMES, 1, CL), jnp.int32),
            pltpu.SMEM((HOMES,), jnp.int32),
            pltpu.VMEM((36, 8, CL), F32),
            pltpu.VMEM((2, 36, 3, 1, CL), F32),
            pltpu.VMEM((36, 8, CL), F32),
            pltpu.VMEM((HOMES, 5, CL, CL), F32),
            pltpu.VMEM((HOMES, 27, 6, CL, CL), F32),
            pltpu.VMEM((HOMES, 3, CL, CL), F32),
            pltpu.VMEM((4, HOMES, 3, 1, CL), F32),
            pltpu.VMEM((1 + len(first), 1, CL), F32),
            pltpu.VMEM((1 + len(second), 1, CL), F32),
            pltpu.SemaphoreType.DMA((5,)),
            pltpu.SemaphoreType.DMA((3,)),
            pltpu.SemaphoreType.DMA((3, 3)),
            pltpu.SemaphoreType.DMA((2,)),
            pltpu.SemaphoreType.DMA((2,)),
        ],
        compiler_params=pltpu.CompilerParams(
            collective_id=0, has_side_effects=True, vmem_limit_bytes=62 * 1024 * 1024
        ),
    )

    def shards(positions, polarity, perm_field, groups, occupancy):
        dipoles, residual = call(
            positions.reshape(HOMES * 3, 1, CL),
            polarity.reshape(HOMES, 1, CL),
            perm_field.reshape(HOMES * 3, 1, CL),
            groups.reshape(HOMES, 1, CL),
            occupancy.reshape(HOMES),
        )
        return dipoles.reshape(positions.shape), residual.reshape(positions.shape)

    return jax.shard_map(
        shards,
        mesh=mesh,
        in_specs=(
            P("gx", "gy", "gz", None, None),
            P("gx", "gy", "gz", None),
            P("gx", "gy", "gz", None, None),
            P("gx", "gy", "gz", None),
            P("gx", "gy", "gz"),
        ),
        out_specs=(P("gx", "gy", "gz", None, None), P("gx", "gy", "gz", None, None)),
        check_vma=False,
    )
```

time: 64.3 us -> 56.5 us (0.88)
  Pallas kernels: 60.2 us -> 53.7 us
  local copies, waits for them, and re-layouts: 3.3 us -> 1.92 us
    pallas_call x1, Pallas kernels: 60.2 us -> 53.7 us  [shards(): call(positions.reshape(HOMES * 3, 1, CL), polarity.reshape(HOMES, 1, CL),...]
    pallas_call x2 -> x0, local copies, waits for them, and re-layouts: 1.16 us -> none
    unnamed x9 -> x6, local copies, waits for them, and re-layouts: 2.13 us -> 1.92 us
where the time goes in v2:
time: 56.5 us; the launch traced here: 56.3 us
  Pallas kernels  53.7 us (95%)
  local copies, waits for them, and re-layouts  1.92 us (3%)
  between operations  0.65 us (1%)
    pallas_call x1, Pallas kernels, shards(): call(positions.reshape(HOMES * 3, 1, CL), polarity.reshape(HOMES, 1, CL),...  53.7 us
    unnamed x6, local copies, waits for them, and re-layouts  1.92 us

profile of v2, /device:TPU:1, one launch (start us, length us, event | category | flops | bytes accessed | tf_op | source)
XLA Modules:
  0.0 56.3 jit_solution(4387639930842806251)
XLA Ops:
  0.6 53.7 %shard_map.68 = (f32[6,1,128]{2,1,0:T(1,128)}, f32[6,1,128]{2,1,0:T(1,128)}) custom-call(f32[6,1,128]{2,1,0:T(1,128)} %bitcast.11, f32[2,1,128]{2,1,0:T(1,128)} %bitcast.15, f32[6,1,128]{2,1,0:T(1,128)} %bitcast.12, s32[2,1,128]{2,1,0:T(1,128)} %bitcast.16, s32[2]{0:T(128)} %bitcast.17), custom_call_target="tpu_custom_call" | custom-call | tf_op jit(solution)/shard_map/pallas_call | solution.py:455
  54.4 0.0 copy-start.1
  54.4 0.7 %copy-done.1 = f32[6,1,128]{2,1,0:T(1,128)S(1)} copy-done((f32[6,1,128]{2,1,0:T(1,128)S(1)}, f32[6,1,128]{2,1,0:T(1,128)}, u32[]{:S(2)}) %copy-start.1) | copy-done | bytes 3096
  55.0 0.0 copy-start
  55.1 0.6 %copy.11 = f32[2,1,1,3,128]{4,2,3,1,0:T(1,128)} copy(f32[2,1,1,3,128]{4,2,3,1,0:T(1,128)S(1)} %bitcast.14) | data formatting | bytes 6144
  55.6 0.1 copy-done
  55.7 0.6 %copy.12 = f32[2,1,1,3,128]{4,2,3,1,0:T(1,128)} copy(f32[2,1,1,3,128]{4,2,3,1,0:T(1,128)S(1)} %bitcast.13) | data formatting | bytes 6144
Async XLA Ops:
  54.4 0.7 %copy-start.1 = (f32[6,1,128]{2,1,0:T(1,128)S(1)}, f32[6,1,128]{2,1,0:T(1,128)}, u32[]{:S(2)}) copy-start(f32[6,1,128]{2,1,0:T(1,128)} %get-tuple-element.4) | copy-start | bytes 9220
  55.0 0.7 %copy-start = (f32[6,1,128]{2,1,0:T(1,128)S(1)}, f32[6,1,128]{2,1,0:T(1,128)}, u32[]{:S(2)}) copy-start(f32[6,1,128]{2,1,0:T(1,128)} %get-tuple-element.5) | copy-start | bytes 9220

commit v3 on v2

--- a/solution.py
+++ b/solution.py
@@ -20,6 +20,7 @@
 BLOCKS = CL // ROWS
 TALL = 64
 TALLS = CL // TALL
+CHUNK = 4
 UNIT = 1.0 / CUTOFF
 LN2 = math.log(2.0)
 TOTAL = 3.0 * UNIT**3
@@ -81,8 +82,7 @@
     perm_ref,
     grp_ref,
     occ_ref,
-    dip_ref,
-    res_ref,
+    out_ref,
     inbox,
     inbox_grp,
     inbox_occ,
@@ -100,6 +100,7 @@
     halo_recv,
     red_send,
     red_recv,
+    greeted,
 ):
     fetches = [
         pltpu.make_async_copy(pos_ref, inbox.at[pl.ds(0, 6)], in_sem.at[0]),
@@ -127,17 +128,15 @@
         )
 
     groups_of = stages(sizes)
-
-    def wrapped(o):
-        return tuple((e + n) % n for e, n in zip(o, sizes))
-
-    peers = list(OFFSETS)
-    known = {wrapped(o) for o in OFFSETS}
-    for stage in groups_of:
-        peers += [o for o in stage if o not in known]
     barrier = pltpu.get_barrier_semaphore()
-    for o in peers:
+    for o in reversed(OFFSETS):
         pl.semaphore_signal(barrier, inc=1, device_id=device(o), device_id_type=MESH)
+
+    def greet(step, reach):
+        for o in (reach, sizes[2] - reach):
+            pl.semaphore_signal(
+                greeted.at[step], inc=1, device_id=device((0, 0, o)), device_id_type=MESH
+            )
 
     lane = lax.broadcasted_iota(jnp.int32, (1, CL), 1)
     eye = lax.broadcasted_iota(jnp.int32, (CL, CL), 0) == lax.broadcasted_iota(
@@ -161,7 +160,7 @@
         halo[h, 3:4, :] = lax.rsqrt(pol)
         halo[h, 7:8, :] = inbox_grp[h].astype(F32)
 
-    pl.semaphore_wait(barrier, len(peers))
+    pl.semaphore_wait(barrier, len(OFFSETS))
 
     def exchange(buf, k):
         for ex, ey, ez in OFFSETS:
@@ -232,14 +231,11 @@
 
     def product(m, v, total):
         xx, yy, zz, xy, xz, yz = m
-        out = (
-            xx * v[0] + xy * v[1] + xz * v[2],
-            xy * v[0] + yy * v[1] + yz * v[2],
-            xz * v[0] + yz * v[1] + zz * v[2],
-        )
-        if total is None:
-            return out
-        return tuple(t + o for t, o in zip(total, out))
+        out = []
+        for a, line in enumerate(((xx, xy, xz), (xy, yy, yz), (xz, yz, zz))):
+            total_a = line[0] * v[0] if total is None else total[a] + line[0] * v[0]
+            out.append((total_a + line[1] * v[1]) + line[2] * v[2])
+        return tuple(out)
 
     def members(group, h):
         if group == 0:
@@ -288,19 +284,20 @@
         shared = (8, 8, 0)[group]
         rim, slot = ((10, 10 + h), (19, 20 + 4 * h), (23, 28 + 4 * h))[group]
         base = (2, 11, 0)[group]
+
+        def step(first, at, count, total):
+            for c in range(count):
+                total = apply(k, h, rows, first + c, at + c, total)
+            return total
+
         if shared:
             total = lax.fori_loop(
                 0,
-                shared,
-                lambda c, t: apply(k, h, rows, base + c, GROUPS[group][0] + c, t),
+                shared // CHUNK,
+                lambda c, t: step(base + CHUNK * c, GROUPS[group][0] + CHUNK * c, CHUNK, t),
                 total,
             )
-        if group == 0:
-            total = apply(k, h, rows, rim, slot, total)
-        else:
-            total = lax.fori_loop(
-                0, 4, lambda c, t: apply(k, h, rows, rim + c, slot + c, t), total
-            )
+        total = step(rim, slot, 1 if group == 0 else 4, total)
         for a in range(3):
             acc[h, a, rows, :] = total[a]
         return unused
@@ -331,6 +328,7 @@
         for slot in range(GROUPS[group][0], sum(GROUPS[group])):
             place(slot)
         lax.fori_loop(0, HOMES * BLOCKS, functools.partial(first_group, group), 0)
+    greet(0, 2)
     image(0)
     for k in range(2):
         exchange(halo_v.at[k], 1 + k)
@@ -338,6 +336,9 @@
         for group in range(3):
             arrived(halo_v.at[k], 1 + k, group)
             lax.fori_loop(0, HOMES * TALLS, functools.partial(later_group, k, group), 0)
+        pl.semaphore_wait(greeted.at[k], 2)
+        if k == 0:
+            greet(1, 4)
         image(1 + k)
 
     row = jnp.zeros((1, CL), F32)
@@ -407,8 +408,8 @@
     for h in range(HOMES):
         for a in range(3):
             v = [basis[k, h, a] for k in range(4)]
-            dip_ref[3 * h + a] = dip[0] * v[0] + dip[1] * v[1] + dip[2] * v[2]
-            res_ref[3 * h + a] = res[0] * v[0] + res[1] * v[1] + res[2] * v[2] + res[3] * v[3]
+            out_ref[3 * h + a] = dip[0] * v[0] + dip[1] * v[1] + dip[2] * v[2]
+            out_ref[6 + 3 * h + a] = res[0] * v[0] + res[1] * v[1] + res[2] * v[2] + res[3] * v[3]
     sent(halo, 0)
     for k in range(2):
         sent(halo_v.at[k], 1 + k)
@@ -420,13 +421,13 @@
 def solution(mesh):
     sizes = tuple(mesh.shape[a] for a in AXES)
     first, second = stages(sizes)
-    vector = jax.ShapeDtypeStruct((HOMES * 3, 1, CL), F32)
+    vector = jax.ShapeDtypeStruct((2 * HOMES * 3, 1, CL), F32)
     vmem = pl.BlockSpec(memory_space=pltpu.VMEM)
     call = pl.pallas_call(
         functools.partial(kernel, sizes),
-        out_shape=(vector, vector),
+        out_shape=vector,
         in_specs=[pl.BlockSpec(memory_space=pl.ANY)] * 5,
-        out_specs=(vmem, vmem),
+        out_specs=vmem,
         scratch_shapes=[
             pltpu.VMEM((14, 1, CL), F32),
             pltpu.VMEM((HOMES, 1, CL), jnp.int32),
@@ -445,6 +446,7 @@
             pltpu.SemaphoreType.DMA((3, 3)),
             pltpu.SemaphoreType.DMA((2,)),
             pltpu.SemaphoreType.DMA((2,)),
+            pltpu.SemaphoreType.REGULAR((2,)),
         ],
         compiler_params=pltpu.CompilerParams(
             collective_id=0, has_side_effects=True, vmem_limit_bytes=62 * 1024 * 1024
@@ -452,14 +454,14 @@
     )
 
     def shards(positions, polarity, perm_field, groups, occupancy):
-        dipoles, residual = call(
+        both = call(
             positions.reshape(HOMES * 3, 1, CL),
             polarity.reshape(HOMES, 1, CL),
             perm_field.reshape(HOMES * 3, 1, CL),
             groups.reshape(HOMES, 1, CL),
             occupancy.reshape(HOMES),
         )
-        return dipoles.reshape(positions.shape), residual.reshape(positions.shape)
+        return both[:6].reshape(positions.shape), both[6:].reshape(positions.shape)
 
     return jax.shard_map(
         shards,

time: 56.5 us -> 52.3 us (0.926)
  Pallas kernels: 53.7 us -> 50.2 us
  local copies, waits for them, and re-layouts: 1.92 us -> 1.26 us
    pallas_call x1, Pallas kernels: 53.7 us -> 50.2 us  [shards(): call(positions.reshape(HOMES * 3, 1, CL), polarity.reshape(HOMES, 1, CL),...]
    unnamed x6 -> x0, local copies, waits for them, and re-layouts: 1.92 us -> none
    slice x0 -> x1, local copies, waits for them, and re-layouts: none -> 1.26 us  [shards(): both[6:].reshape(positions.shape)]
where the time goes in v3:
time: 52.3 us; the launch traced here: 52.1 us
  Pallas kernels  50.2 us (96%)
  local copies, waits for them, and re-layouts  1.26 us (2%)
  between operations  0.64 us (1%)
    pallas_call x1, Pallas kernels, shards(): call(positions.reshape(HOMES * 3, 1, CL), polarity.reshape(HOMES, 1, CL),...  50.2 us
    slice x1, local copies, waits for them, and re-layouts, shards(): both[6:].reshape(positions.shape)  1.26 us

profile of v3, /device:TPU:1, one launch (start us, length us, event | category | flops | bytes accessed | tf_op | source)
XLA Modules:
  0.0 52.1 jit_solution(8108675544958048693)
XLA Ops:
  0.6 50.2 %shard_map.68 = f32[12,1,128]{2,1,0:T(1,128)} custom-call(f32[6,1,128]{2,1,0:T(1,128)} %bitcast.13, f32[2,1,128]{2,1,0:T(1,128)} %bitcast.15, f32[6,1,128]{2,1,0:T(1,128)} %bitcast.14, s32[2,1,128]{2,1,0:T(1,128)} %bitcast.16, s32[2]{0:T(128)} %bitcast.17), custom_call_target="tpu_custom_call" | custom-call | tf_op jit(solution)/shard_map/pallas_call | solution.py:457
  50.9 1.3 %fusion = (f32[6,1,128]{2,1,0:T(1,128)}, f32[6,1,128]{2,1,0:T(1,128)}) fusion(f32[12,1,128]{2,1,0:T(1,128)} %shard_map.68), kind=kLoop, calls=%fused_computation | loop fusion | bytes 12288 | tf_op jit(solution)/shard_map/slice | solution.py:464

commit v4 on v3

--- a/solution.py
+++ b/solution.py
@@ -23,6 +23,7 @@
 CHUNK = 4
 UNIT = 1.0 / CUTOFF
 LN2 = math.log(2.0)
+TINY = 1e-36
 TOTAL = 3.0 * UNIT**3
 F32 = jnp.float32
 
@@ -51,7 +52,7 @@
         for ez in (-1, 0, 1)
         if (ex, ey, ez) != (0, 0, 0)
     ],
-    key=lambda o: -sum(abs(e) for e in o),
+    key=lambda o: sum(abs(e) for e in o),
 )
 
 
@@ -70,9 +71,12 @@
 
 
 def stages(sizes):
+    def way(o):
+        return -sum(min(e, n - e) for e, n in zip(o, sizes))
+
     first = [(i, j, 0) for i in range(sizes[0]) for j in range(sizes[1]) if (i, j) != (0, 0)]
     second = [(0, 0, k) for k in range(1, sizes[2])]
-    return (first, second)
+    return (sorted(first, key=way), sorted(second, key=way))
 
 
 def kernel(
@@ -129,7 +133,7 @@
 
     groups_of = stages(sizes)
     barrier = pltpu.get_barrier_semaphore()
-    for o in reversed(OFFSETS):
+    for o in OFFSETS:
         pl.semaphore_signal(barrier, inc=1, device_id=device(o), device_id_type=MESH)
 
     def greet(step, reach):
@@ -196,46 +200,42 @@
                 add = jnp.where(sub == a, jnp.float32(PLACES[slot][a] * CELL_EDGE * UNIT), add)
         staged[slot] = halo[slot] + add
 
-    def couple(h, i, n, slot, total, own):
-        rows = pl.ds(pl.multiple_of(i * ROWS, ROWS), ROWS)
+    def couple_tile(h, first, n, slot, total, own):
+        rows = pl.ds(first, 8)
         r = [staged[slot, a : a + 1, :] - home[h, a, rows, :] for a in range(3)]
         d2 = r[0] * r[0] + r[1] * r[1] + r[2] * r[2]
         if own:
-            diagonal = lax.broadcasted_iota(jnp.int32, (ROWS, CL), 0) + i * ROWS
-            diagonal = diagonal == lax.broadcasted_iota(jnp.int32, (ROWS, CL), 1)
+            diagonal = lax.broadcasted_iota(jnp.int32, (8, CL), 0) + first
+            diagonal = diagonal == lax.broadcasted_iota(jnp.int32, (8, CL), 1)
             d2 = d2 + diagonal.astype(F32)
         inv = lax.rsqrt(d2)
-        inv2 = inv * inv
         taper = jnp.maximum(1.0 - d2, 0.0)
-        g = (taper * taper) * (inv2 * inv)
+        scaled = taper * inv
+        g = (scaled * scaled) * inv
         if own:
             g = jnp.where(staged[slot, 7:8, :] != home[h, 4, rows, :], g, 0.0)
         t = (d2 * d2 * inv) * (home[h, 3, rows, :] * staged[slot, 3:4, :])
-        falloff = jnp.exp2(t)
-        ge = g * falloff
+        ge = g * jnp.exp2(t)
         c3 = g - ge
-        c5 = (c3 + (LN2 * t) * ge) * inv2
-        c3 = c3 * (1.0 / 3.0)
-        p = [c5 * r[a] for a in range(3)]
-        m = (
-            p[0] * r[0] - c3,
-            p[1] * r[1] - c3,
-            p[2] * r[2] - c3,
-            p[0] * r[1],
-            p[0] * r[2],
-            p[1] * r[2],
-        )
-        for c in range(6):
+        z = jnp.maximum(c3 + (LN2 * t) * ge, TINY)
+        f = (z * lax.rsqrt(z)) * inv
+        m = (f * r[0], f * r[1], f * r[2], c3 * (1.0 / 3.0))
+        for c in range(4):
             tens[h, n, c, rows, :] = m[c]
         return product(m, [staged[slot, 4 + a : 5 + a, :] for a in range(3)], total)
 
+    def couple(h, i, n, slot, total, own):
+        out = []
+        for tile in range(ROWS // 8):
+            first = pl.multiple_of(i * ROWS + 8 * tile, 8)
+            part = None if total is None else total[3 * tile : 3 * tile + 3]
+            out += couple_tile(h, first, n, slot, part, own)
+        return tuple(out)
+
     def product(m, v, total):
-        xx, yy, zz, xy, xz, yz = m
-        out = []
-        for a, line in enumerate(((xx, xy, xz), (xy, yy, yz), (xz, yz, zz))):
-            total_a = line[0] * v[0] if total is None else total[a] + line[0] * v[0]
-            out.append((total_a + line[1] * v[1]) + line[2] * v[2])
-        return tuple(out)
+        s = m[0] * v[0] + m[1] * v[1] + m[2] * v[2]
+        out = [m[a] * s - m[3] * v[a] for a in range(3)]
+        return tuple(out if total is None else (t + o for t, o in zip(total, out)))
 
     def members(group, h):
         if group == 0:
@@ -248,46 +248,55 @@
         h, i = it // BLOCKS, it % BLOCKS
         total = couple(h, i, 0, h, None, True)
         total = couple(h, i, 1, 1 - h, total, False)
-        rows = pl.ds(pl.multiple_of(i * ROWS, ROWS), ROWS)
-        for a in range(3):
-            acc[h, a, rows, :] = total[a]
+        closed(h, i * ROWS, total)
         return unused
 
     def first_group(group, it, unused):
         h, i = it // BLOCKS, it % BLOCKS
-        rows = pl.ds(pl.multiple_of(i * ROWS, ROWS), ROWS)
-        total = tuple(acc[h, a, rows, :] for a in range(3))
+        total = opened(h, i * ROWS, ROWS)
         for n, slot in members(group, h):
             total = couple(h, i, n, slot, total, False)
-        for a in range(3):
-            acc[h, a, rows, :] = total[a]
+        closed(h, i * ROWS, total)
         return unused
 
-    def apply(k, h, rows, n, slot, total):
-        return product(
-            [tens[h, n, c, rows, :] for c in range(6)], [halo_v[k, slot, a] for a in range(3)], total
+    def apply(k, h, first, n, slot, total):
+        v = [halo_v[k, slot, a] for a in range(3)]
+        out = []
+        for tile in range(TALL // 8):
+            rows = pl.ds(pl.multiple_of(first + 8 * tile, 8), 8)
+            part = None if total is None else total[3 * tile : 3 * tile + 3]
+            out += product([tens[h, n, c, rows, :] for c in range(4)], v, part)
+        return tuple(out)
+
+    def opened(h, first, tall):
+        return tuple(
+            acc[h, a, pl.ds(pl.multiple_of(first + 8 * tile, 8), 8), :]
+            for tile in range(tall // 8)
+            for a in range(3)
         )
 
+    def closed(h, first, total):
+        for tile in range(len(total) // 3):
+            for a in range(3):
+                acc[h, a, pl.ds(pl.multiple_of(first + 8 * tile, 8), 8), :] = total[3 * tile + a]
+
     def later_own(k, it, unused):
-        h, i = it // TALLS, it % TALLS
-        rows = pl.ds(pl.multiple_of(i * TALL, TALL), TALL)
-        total = apply(k, h, rows, 0, h, None)
-        total = apply(k, h, rows, 1, 1 - h, total)
-        for a in range(3):
-            acc[h, a, rows, :] = total[a]
+        h, first = it // TALLS, it % TALLS * TALL
+        total = apply(k, h, first, 0, h, None)
+        total = apply(k, h, first, 1, 1 - h, total)
+        closed(h, first, total)
         return unused
 
     def later_group(k, group, it, unused):
-        h, i = it // TALLS, it % TALLS
-        rows = pl.ds(pl.multiple_of(i * TALL, TALL), TALL)
-        total = tuple(acc[h, a, rows, :] for a in range(3))
+        h, first = it // TALLS, it % TALLS * TALL
+        total = opened(h, first, TALL)
         shared = (8, 8, 0)[group]
         rim, slot = ((10, 10 + h), (19, 20 + 4 * h), (23, 28 + 4 * h))[group]
         base = (2, 11, 0)[group]
 
-        def step(first, at, count, total):
+        def step(n, at, count, total):
             for c in range(count):
-                total = apply(k, h, rows, first + c, at + c, total)
+                total = apply(k, h, first, n + c, at + c, total)
             return total
 
         if shared:
@@ -298,8 +307,7 @@
                 total,
             )
         total = step(rim, slot, 1 if group == 0 else 4, total)
-        for a in range(3):
-            acc[h, a, rows, :] = total[a]
+        closed(h, first, total)
         return unused
 
     def image(k):
@@ -436,7 +444,7 @@
             pltpu.VMEM((2, 36, 3, 1, CL), F32),
             pltpu.VMEM((36, 8, CL), F32),
             pltpu.VMEM((HOMES, 5, CL, CL), F32),
-            pltpu.VMEM((HOMES, 27, 6, CL, CL), F32),
+            pltpu.VMEM((HOMES, 27, 4, CL, CL), F32),
             pltpu.VMEM((HOMES, 3, CL, CL), F32),
             pltpu.VMEM((4, HOMES, 3, 1, CL), F32),
             pltpu.VMEM((1 + len(first), 1, CL), F32),
@@ -449,7 +457,7 @@
             pltpu.SemaphoreType.REGULAR((2,)),
         ],
         compiler_params=pltpu.CompilerParams(
-            collective_id=0, has_side_effects=True, vmem_limit_bytes=62 * 1024 * 1024
+            collective_id=0, has_side_effects=True, vmem_limit_bytes=32 * 1024 * 1024
         ),
     )
 

time: 52.3 us -> 49.6 us (0.948)
  Pallas kernels: 50.2 us -> 47.5 us
    pallas_call x1, Pallas kernels: 50.2 us -> 47.5 us  [shards(): call(positions.reshape(HOMES * 3, 1, CL), polarity.reshape(HOMES, 1, CL),...]
    unnamed x0 -> x10, local copies, waits for them, and re-layouts: none -> 0.69 us
    slice x1, local copies, waits for them, and re-layouts: 1.26 us -> 0.59 us  [shards(): both[6:].reshape(positions.shape)]
where the time goes in v4:
time: 49.6 us; the launch traced here: 49.5 us
  Pallas kernels  47.5 us (96%)
  local copies, waits for them, and re-layouts  1.27 us (3%)
  between operations  0.68 us (1%)
    pallas_call x1, Pallas kernels, shards(): call(positions.reshape(HOMES * 3, 1, CL), polarity.reshape(HOMES, 1, CL),...  47.5 us

profile of v4, /device:TPU:1, one launch (start us, length us, event | category | flops | bytes accessed | tf_op | source)
XLA Modules:
  0.0 49.5 jit_solution(1395217355228113690)
XLA Ops:
  0.6 0.0 copy-start.3
  0.6 0.0 copy-start.1
  0.7 0.0 copy-start
  0.7 0.0 copy-start.2
  0.7 0.0 copy-start.4
  0.7 0.6 %copy-done.3 = s32[2,1,1,128]{3,2,1,0:T(1,128)S(1)} copy-done((s32[2,1,1,128]{3,2,1,0:T(1,128)S(1)}, s32[2,1,1,128]{3,2,1,0:T(1,128)}, u32[]{:S(2)}) %copy-start.3) | copy-done | bytes 1048
  1.3 0.0 copy-done.1
  1.3 0.0 copy-done
  1.3 0.0 copy-done.2
  1.4 0.0 copy-done.4
  1.4 47.5 %shard_map.68 = f32[12,1,128]{2,1,0:T(1,128)S(1)} custom-call(f32[6,1,128]{2,1,0:T(1,128)S(1)} %bitcast.11, f32[2,1,128]{2,1,0:T(1,128)S(1)} %bitcast.13, f32[6,1,128]{2,1,0:T(1,128)S(1)} %bitcast.12, s32[2,1,128]{2,1,0:T(1,128)S(1)} %bitcast.14, s32[2]{0:T(128)S(1)} %bitcast.15), custom_call_target="tpu_custom_call" | custom-call | tf_op jit(solution)/shard_map/pallas_call | solution.py:465
  48.9 0.6 %fusion = (f32[6,1,128]{2,1,0:T(1,128)}, f32[6,1,128]{2,1,0:T(1,128)}) fusion(f32[12,1,128]{2,1,0:T(1,128)S(1)} %shard_map.68), kind=kLoop, calls=%fused_computation | loop fusion | bytes 12288 | tf_op jit(solution)/shard_map/slice | solution.py:472
Async XLA Ops:
  0.6 0.7 %copy-start.3 = (s32[2,1,1,128]{3,2,1,0:T(1,128)S(1)}, s32[2,1,1,128]{3,2,1,0:T(1,128)}, u32[]{:S(2)}) copy-start(s32[2,1,1,128]{3,2,1,0:T(1,128)} %param.8) | copy-start | bytes 3076
  0.6 0.7 %copy-start.1 = (f32[2,1,1,3,128]{4,2,3,1,0:T(1,128)S(1)}, f32[2,1,1,3,128]{4,2,3,1,0:T(1,128)}, u32[]{:S(2)}) copy-start(f32[2,1,1,3,128]{4,2,3,1,0:T(1,128)} %param.7) | copy-start | bytes 9220
  0.7 0.7 %copy-start = (f32[2,1,1,3,128]{4,2,3,1,0:T(1,128)S(1)}, f32[2,1,1,3,128]{4,2,3,1,0:T(1,128)}, u32[]{:S(2)}) copy-start(f32[2,1,1,3,128]{4,2,3,1,0:T(1,128)} %param.5) | copy-start | bytes 9220
  0.7 0.7 %copy-start.2 = (f32[2,1,1,128]{3,2,1,0:T(1,128)S(1)}, f32[2,1,1,128]{3,2,1,0:T(1,128)}, u32[]{:S(2)}) copy-start(f32[2,1,1,128]{3,2,1,0:T(1,128)} %param.6) | copy-start | bytes 3076
  0.7 0.7 %copy-start.4 = (s32[2,1,1]{0,2,1:T(1,128)S(1)}, s32[2,1,1]{0,2,1:T(1,128)}, u32[]{:S(2)}) copy-start(s32[2,1,1]{0,2,1:T(1,128)} %param.9) | copy-start | bytes 28

commit v5 on v4

--- a/solution.py
+++ b/solution.py
@@ -96,6 +96,7 @@
     home,
     tens,
     acc,
+    spare,
     basis,
     red_a,
     red_b,
@@ -310,6 +311,44 @@
         closed(h, first, total)
         return unused
 
+    def half_own(k, it, unused):
+        h, first = it // TALLS, it % TALLS * TALL
+        total = apply(k, h, first, 0, h, None)
+        total = apply(k, h, first, 1, 1 - h, total)
+        total = tuple(0.5 * t for t in total)
+        closed(h, first, total)
+        for tile in range(len(total) // 3):
+            for a in range(3):
+                spare[h, a, pl.ds(pl.multiple_of(first + 8 * tile, 8), 8), :] = total[3 * tile + a]
+        return unused
+
+    def half_group(k, cells, it, unused):
+        h, first = it // TALLS, it % TALLS * TALL
+        total = opened(h, first, TALL)
+        for n, slot in cells:
+            total = apply(k, h, first, n, slot, total)
+        closed(h, first, total)
+        return unused
+
+    def half_rim(k, group, h, i, unused):
+        total = opened(h, i * TALL, TALL)
+        n, slot, count = ((10, 10 + h, 1), (19, 20 + 4 * h, 4), (23, 28 + 4 * h, 4))[group]
+        for c in range(count):
+            total = apply(k, h, i * TALL, n + c, slot + c, total)
+        closed(h, i * TALL, total)
+        return unused
+
+    def half(k, part, group):
+        cells = (
+            ([(n, n) for n in (4, 5, 8, 9)], [(n - 1, n) for n in range(16, 20)]),
+            ([(n, n) for n in (2, 3, 6, 7)], [(n - 1, n) for n in range(12, 16)]),
+        )[part]
+        if group < 2:
+            lax.fori_loop(
+                0, HOMES * TALLS, functools.partial(half_group, k, cells[group]), 0
+            )
+        lax.fori_loop(0, TALLS, functools.partial(half_rim, k, group, 1 - part), 0)
+
     def image(k):
         for h in range(HOMES):
             for a in range(3):
@@ -338,25 +377,45 @@
         lax.fori_loop(0, HOMES * BLOCKS, functools.partial(first_group, group), 0)
     greet(0, 2)
     image(0)
-    for k in range(2):
-        exchange(halo_v.at[k], 1 + k)
-        lax.fori_loop(0, HOMES * TALLS, functools.partial(later_own, k), 0)
-        for group in range(3):
-            arrived(halo_v.at[k], 1 + k, group)
-            lax.fori_loop(0, HOMES * TALLS, functools.partial(later_group, k, group), 0)
-        pl.semaphore_wait(greeted.at[k], 2)
-        if k == 0:
-            greet(1, 4)
-        image(1 + k)
+    exchange(halo_v.at[0], 1)
+    lax.fori_loop(0, HOMES * TALLS, functools.partial(later_own, 0), 0)
+    for group in range(3):
+        arrived(halo_v.at[0], 1, group)
+        lax.fori_loop(0, HOMES * TALLS, functools.partial(later_group, 0, group), 0)
+    pl.semaphore_wait(greeted.at[0], 2)
+    greet(1, 4)
+    image(1)
+    exchange(halo_v.at[1], 2)
+    vectors = [[basis[2, h, a] for a in range(3)] for h in range(HOMES)]
+    filler = [jnp.zeros((1, CL), F32)] * 2
+    cols = jnp.transpose(jnp.concatenate(vectors[0] + vectors[1] + filler, axis=0))
+    for h in range(HOMES):
+        for a in range(3):
+            home[h, a] = jnp.broadcast_to(cols[:, 3 * h + a : 3 * h + a + 1], (CL, CL))
+    lax.fori_loop(0, HOMES * TALLS, functools.partial(half_own, 1), 0)
 
     row = jnp.zeros((1, CL), F32)
-    for m in range(6):
+    for m in range(5):
         part = jnp.zeros((1, CL), F32)
         for h in range(HOMES):
             for a in range(3):
                 part = part + basis[m // 2, h, a] * basis[(m + 1) // 2, h, a]
         row = jnp.where(lane == m, jnp.sum(part, axis=1, keepdims=True), row)
-
+    part = jnp.zeros((1, CL), F32)
+    for h in range(HOMES):
+        for v in vectors[h]:
+            part = part + v * v * (live[h] * invpol[h] - SHIFT)
+    for group in range(3):
+        arrived(halo_v.at[1], 2, group)
+        half(1, 0, group)
+    inner = jnp.zeros((CL, CL), F32)
+    for h in range(HOMES):
+        for a in range(3):
+            inner = inner + home[h, a] * acc[h, a]
+    part = part - (2.0 * TOTAL) * jnp.sum(inner, axis=0, keepdims=True)
+    row = jnp.where(lane == 5, jnp.sum(part, axis=1, keepdims=True), row)
+
+    pl.semaphore_wait(greeted.at[1], 2)
     for s, (stage, buf) in enumerate(zip(groups_of, (red_a, red_b))):
         buf[0] = row
         for i, o in enumerate(stage):
@@ -368,6 +427,13 @@
                 device_id=device(o),
                 device_id_type=MESH,
             ).start()
+        if s == 0:
+            for h in range(HOMES):
+                for a in range(3):
+                    acc[h, a] = acc[h, a] + spare[h, a]
+            for group in range(3):
+                half(1, 1, group)
+            image(2)
         region = buf.at[pl.ds(1, len(stage))]
         pltpu.make_async_copy(region, region, red_recv.at[s]).wait()
         parts = [buf[i] for i in range(1 + len(stage))]
@@ -446,6 +512,7 @@
             pltpu.VMEM((HOMES, 5, CL, CL), F32),
             pltpu.VMEM((HOMES, 27, 4, CL, CL), F32),
             pltpu.VMEM((HOMES, 3, CL, CL), F32),
+            pltpu.VMEM((HOMES, 3, CL, CL), F32),
             pltpu.VMEM((4, HOMES, 3, 1, CL), F32),
             pltpu.VMEM((1 + len(first), 1, CL), F32),
             pltpu.VMEM((1 + len(second), 1, CL), F32),

time: 49.6 us -> 48.9 us (0.986)
  Pallas kernels: 47.5 us -> 46.8 us
    pallas_call x1, Pallas kernels: 47.5 us -> 46.8 us  [shards(): call(positions.reshape(HOMES * 3, 1, CL), polarity.reshape(HOMES, 1, CL),...]
where the time goes in v5:
time: 48.9 us; the launch traced here: 48.7 us
  Pallas kernels  46.8 us (96%)
  local copies, waits for them, and re-layouts  1.27 us (3%)
  between operations  0.68 us (1%)
    pallas_call x1, Pallas kernels, shards(): call(positions.reshape(HOMES * 3, 1, CL), polarity.reshape(HOMES, 1, CL),...  46.8 us

profile of v5, /device:TPU:1, one launch (start us, length us, event | category | flops | bytes accessed | tf_op | source)
XLA Modules:
  0.0 48.7 jit_solution(5604223631965570051)
XLA Ops:
  0.6 0.0 copy-start.3
  0.6 0.0 copy-start.1
  0.7 0.0 copy-start
  0.7 0.0 copy-start.2
  0.7 0.0 copy-start.4
  0.7 0.6 %copy-done.3 = s32[2,1,1,128]{3,2,1,0:T(1,128)S(1)} copy-done((s32[2,1,1,128]{3,2,1,0:T(1,128)S(1)}, s32[2,1,1,128]{3,2,1,0:T(1,128)}, u32[]{:S(2)}) %copy-start.3) | copy-done | bytes 1048
  1.3 0.0 copy-done.1
  1.3 0.0 copy-done
  1.3 0.0 copy-done.2
  1.4 0.0 copy-done.4
  1.4 46.8 %shard_map.68 = f32[12,1,128]{2,1,0:T(1,128)S(1)} custom-call(f32[6,1,128]{2,1,0:T(1,128)S(1)} %bitcast.11, f32[2,1,128]{2,1,0:T(1,128)S(1)} %bitcast.13, f32[6,1,128]{2,1,0:T(1,128)S(1)} %bitcast.12, s32[2,1,128]{2,1,0:T(1,128)S(1)} %bitcast.14, s32[2]{0:T(128)S(1)} %bitcast.15), custom_call_target="tpu_custom_call" | custom-call | tf_op jit(solution)/shard_map/pallas_call | solution.py:532
  48.1 0.6 %fusion = (f32[6,1,128]{2,1,0:T(1,128)}, f32[6,1,128]{2,1,0:T(1,128)}) fusion(f32[12,1,128]{2,1,0:T(1,128)S(1)} %shard_map.68), kind=kLoop, calls=%fused_computation | loop fusion | bytes 12288 | tf_op jit(solution)/shard_map/slice | solution.py:539
Async XLA Ops:
  0.6 0.7 %copy-start.3 = (s32[2,1,1,128]{3,2,1,0:T(1,128)S(1)}, s32[2,1,1,128]{3,2,1,0:T(1,128)}, u32[]{:S(2)}) copy-start(s32[2,1,1,128]{3,2,1,0:T(1,128)} %param.8) | copy-start | bytes 3076
  0.6 0.7 %copy-start.1 = (f32[2,1,1,3,128]{4,2,3,1,0:T(1,128)S(1)}, f32[2,1,1,3,128]{4,2,3,1,0:T(1,128)}, u32[]{:S(2)}) copy-start(f32[2,1,1,3,128]{4,2,3,1,0:T(1,128)} %param.7) | copy-start | bytes 9220
  0.7 0.7 %copy-start = (f32[2,1,1,3,128]{4,2,3,1,0:T(1,128)S(1)}, f32[2,1,1,3,128]{4,2,3,1,0:T(1,128)}, u32[]{:S(2)}) copy-start(f32[2,1,1,3,128]{4,2,3,1,0:T(1,128)} %param.5) | copy-start | bytes 9220
  0.7 0.7 %copy-start.2 = (f32[2,1,1,128]{3,2,1,0:T(1,128)S(1)}, f32[2,1,1,128]{3,2,1,0:T(1,128)}, u32[]{:S(2)}) copy-start(f32[2,1,1,128]{3,2,1,0:T(1,128)} %param.6) | copy-start | bytes 3076
  0.7 0.7 %copy-start.4 = (s32[2,1,1]{0,2,1:T(1,128)S(1)}, s32[2,1,1]{0,2,1:T(1,128)}, u32[]{:S(2)}) copy-start(s32[2,1,1]{0,2,1:T(1,128)} %param.9) | copy-start | bytes 28

commit v6 on v5

--- a/solution.py
+++ b/solution.py
@@ -114,8 +114,6 @@
         pltpu.make_async_copy(grp_ref, inbox_grp, in_sem.at[3]),
         pltpu.make_async_copy(occ_ref, inbox_occ, in_sem.at[4]),
     ]
-    for c in fetches:
-        c.start()
 
     here = tuple(lax.axis_index(a) for a in AXES)
     near = [
@@ -136,6 +134,8 @@
     barrier = pltpu.get_barrier_semaphore()
     for o in OFFSETS:
         pl.semaphore_signal(barrier, inc=1, device_id=device(o), device_id_type=MESH)
+    for c in fetches:
+        c.start()
 
     def greet(step, reach):
         for o in (reach, sizes[2] - reach):
@@ -529,13 +529,14 @@
     )
 
     def shards(positions, polarity, perm_field, groups, occupancy):
-        both = call(
+        inputs = (
             positions.reshape(HOMES * 3, 1, CL),
             polarity.reshape(HOMES, 1, CL),
             perm_field.reshape(HOMES * 3, 1, CL),
             groups.reshape(HOMES, 1, CL),
             occupancy.reshape(HOMES),
         )
+        both = call(*[pltpu.with_memory_space_constraint(v, pltpu.HBM) for v in inputs])
         return both[:6].reshape(positions.shape), both[6:].reshape(positions.shape)
 
     return jax.shard_map(

time: 48.9 us -> 48.1 us (0.984)
  local copies, waits for them, and re-layouts: 1.27 us -> 0.59 us
    unnamed x10 -> x0, local copies, waits for them, and re-layouts: 0.69 us -> none
where the time goes in v6:
time: 48.1 us; the launch traced here: 48 us
  Pallas kernels  46.8 us (97%)
  between operations  0.64 us (1%)
  local copies, waits for them, and re-layouts  0.59 us (1%)
    pallas_call x1, Pallas kernels, shards(): call(*[pltpu.with_memory_space_constraint(v, pltpu.HBM) for v in inputs])  46.8 us

profile of v6, /device:TPU:1, one launch (start us, length us, event | category | flops | bytes accessed | tf_op | source)
XLA Modules:
  0.0 48.0 jit_solution(3733867064941245233)
XLA Ops:
  0.6 46.8 %shard_map.68 = f32[12,1,128]{2,1,0:T(1,128)S(1)} custom-call(f32[6,1,128]{2,1,0:T(1,128)} %bitcast.13, f32[2,1,128]{2,1,0:T(1,128)} %bitcast.15, f32[6,1,128]{2,1,0:T(1,128)} %bitcast.14, s32[2,1,128]{2,1,0:T(1,128)} %bitcast.16, s32[2]{0:T(128)} %bitcast.17), custom_call_target="tpu_custom_call" | custom-call | tf_op jit(solution)/shard_map/pallas_call | solution.py:539
  47.4 0.6 %fusion = (f32[6,1,128]{2,1,0:T(1,128)}, f32[6,1,128]{2,1,0:T(1,128)}) fusion(f32[12,1,128]{2,1,0:T(1,128)S(1)} %shard_map.68), kind=kLoop, calls=%fused_computation | loop fusion | bytes 12288 | tf_op jit(solution)/shard_map/slice | solution.py:540

commit v7 on v6

--- a/solution.py
+++ b/solution.py
@@ -375,17 +375,17 @@
         for slot in range(GROUPS[group][0], sum(GROUPS[group])):
             place(slot)
         lax.fori_loop(0, HOMES * BLOCKS, functools.partial(first_group, group), 0)
-    greet(0, 2)
     image(0)
     exchange(halo_v.at[0], 1)
+    greet(0, 2)
     lax.fori_loop(0, HOMES * TALLS, functools.partial(later_own, 0), 0)
     for group in range(3):
         arrived(halo_v.at[0], 1, group)
         lax.fori_loop(0, HOMES * TALLS, functools.partial(later_group, 0, group), 0)
+    image(1)
+    exchange(halo_v.at[1], 2)
     pl.semaphore_wait(greeted.at[0], 2)
     greet(1, 4)
-    image(1)
-    exchange(halo_v.at[1], 2)
     vectors = [[basis[2, h, a] for a in range(3)] for h in range(HOMES)]
     filler = [jnp.zeros((1, CL), F32)] * 2
     cols = jnp.transpose(jnp.concatenate(vectors[0] + vectors[1] + filler, axis=0))

time: 48.1 us -> 48 us (level)
  no operation moved by 1% of the time
where the time goes in v7:
time: 48 us; the launch traced here: 47.9 us
  Pallas kernels  46.6 us (97%)
  between operations  0.64 us (1%)
  local copies, waits for them, and re-layouts  0.59 us (1%)
    pallas_call x1, Pallas kernels, shards(): call(*[pltpu.with_memory_space_constraint(v, pltpu.HBM) for v in inputs])  46.6 us

profile of v7, /device:TPU:1, one launch (start us, length us, event | category | flops | bytes accessed | tf_op | source)
XLA Modules:
  0.0 47.9 jit_solution(13520769455599661722)
XLA Ops:
  0.6 46.6 %shard_map.68 = f32[12,1,128]{2,1,0:T(1,128)S(1)} custom-call(f32[6,1,128]{2,1,0:T(1,128)} %bitcast.13, f32[2,1,128]{2,1,0:T(1,128)} %bitcast.15, f32[6,1,128]{2,1,0:T(1,128)} %bitcast.14, s32[2,1,128]{2,1,0:T(1,128)} %bitcast.16, s32[2]{0:T(128)} %bitcast.17), custom_call_target="tpu_custom_call" | custom-call | tf_op jit(solution)/shard_map/pallas_call | solution.py:539
  47.3 0.6 %fusion = (f32[6,1,128]{2,1,0:T(1,128)}, f32[6,1,128]{2,1,0:T(1,128)}) fusion(f32[12,1,128]{2,1,0:T(1,128)S(1)} %shard_map.68), kind=kLoop, calls=%fused_computation | loop fusion | bytes 12288 | tf_op jit(solution)/shard_map/slice | solution.py:540
